TPU v7x, 128 devices: a whole 4x4x4 slice. The times are simulated.
128 devices in a mesh: marker: 4 (over z_hi, core), animal: 32 (over x, y, z_lo).
Axes of the slice: x: 4, y: 4, z: 4 (z_hi: 2, z_lo: 2; z = z_hi * 2 + z_lo), core: 2. Of those that a mesh axis runs over, the one named last changes fastest.
Arguments:
- genotypes: int32 [24576, 32768], P('animal', 'marker'), may hold values from 0 to 2
- frequencies: bfloat16 [32768, 512], P('marker'), may hold values from -0.0625 to 0.0625
- phases: float32 [512], replicated, may hold values from -3.140625 to 3.140625
- phenotypes: bfloat16 [24576, 64], P('animal'), may hold values from -6 to 6
Outputs:
- gram: float32 [512, 512], P('animal')
- cross: float32 [512, 64], P('animal')
All inputs are finite; a program needn't handle non-finite values.
Results may differ from a plain program's by a relative error of at most 0.0029.
Values may be sent and summed in bfloat16 or wider, within the bound.
No kernel may reach another device: no remote copies, remote signals or barrier semaphores. Data moves between devices by JAX's collectives and lax.ppermute only.
A program may use at most 128 MiB of HBM per device.

v0:
```python
import math

import jax
import jax.numpy as jnp
from jax import lax
from jax.sharding import PartitionSpec as P


def on_device(genotypes, frequencies, phases, phenotypes):
    local_rows = genotypes.shape[0]
    feat_count = frequencies.shape[1]
    animals_all = float(lax.axis_size("animal") * local_rows)
    dosage = (genotypes - 1).astype(jnp.bfloat16)
    partial_value = jnp.dot(dosage, frequencies, preferred_element_type=jnp.float32)
    projection = lax.psum(partial_value, "marker")
    features = (math.sqrt(2.0) * jnp.cos(projection + phases)).astype(jnp.bfloat16)
    right_side = jnp.concatenate([features, phenotypes], axis=1)
    reduced = lax.psum_scatter(
        lax.dot_general(
            features, right_side, (((0,), (0,)), ((), ())), preferred_element_type=jnp.float32
        ),
        "animal",
        scatter_dimension=0,
        tiled=True,
    )
    gram_rows = reduced[:, :feat_count]
    cross_rows = reduced[:, feat_count:]
    return (gram_rows / animals_all, cross_rows / math.sqrt(animals_all))


def solution(mesh):
    in_specs = (P("animal", "marker"), P("marker", None), P(), P("animal", None))
    out_specs = (P("animal", None), P("animal", None))
    return jax.shard_map(
        on_device, mesh=mesh, in_specs=in_specs, out_specs=out_specs, check_vma=False
    )
```

profile of v0, /device:TPU:0, one launch (start us, length us, event | category | flops | bytes accessed | tf_op | source)
XLA Modules:
  0.0 254.7 jit_solution(3881698247868267979)
XLA Ops:
  7.2 0.0 copy-start
  7.2 0.0 copy-start.1
  7.2 0.0 all-reduce.2.cloned.1.call-start
  7.2 14.9 %fusion = f32[768,512]{1,0:T(8,128)} fusion(bf16[8192,512]{1,0:T(8,128)(2,1)} %param.5, s32[768,8192]{1,0:T(8,128)} %param.4), kind=kOutput, calls=%fused_computation.1 | convolution fusion | flops 6455033856 | bytes 35127296 | tf_op jit(solution)/shard_map/dot_general | solution.py:14
  22.1 0.0 all-reduce.2.cloned.1.call-update
  22.1 0.0 reduce-scatter.2.cloned.1.call-start
  22.2 0.0 copy-done
  22.2 0.2 copy.6
  22.4 53.7 %all-reduce.2.cloned.1.call-done = f32[768,512]{1,0:T(8,128)} async-done(((f32[768,512]{1,0:T(8,128)}), f32[768,512]{1,0:T(8,128)}) %all-reduce.2.cloned.1.call-update) | async-done | bytes 1572880 | tf_op jit(solution)/shard_map/psum | solution.py:15
  76.0 0.0 copy-done.1
  76.0 6.2 %multiply_convert_fusion = bf16[768,512]{1,0:T(8,128)(2,1)S(1)} fusion(f32[768,512]{1,0:T(8,128)} %all-reduce.2.cloned.1.call-done, f32[512]{0:T(512)S(1)} %copy-done.1), kind=kLoop, calls=%fused_computation.3 | loop fusion | flops 1179648 | bytes 2361344 | tf_op jit(solution)/shard_map/convert_element_type | solution.py:16
  82.2 1.9 fusion.2
  84.1 0.0 reduce-scatter.2.cloned.1.call-update
  84.1 161.1 %reduce-scatter.2.cloned.1.call-done = f32[16,576]{1,0:T(8,128)} async-done(((f32[512,576]{1,0:T(8,128)}), f32[16,576]{1,0:T(8,128)}) %reduce-scatter.2.cloned.1.call-update) | async-done | bytes 36880 | tf_op jit(solution)/shard_map/reduce_scatter | solution.py:18
  245.2 1.4 slice_multiply_fusion
  246.6 1.3 slice_multiply_fusion.1
Async XLA Ops:
  7.2 15.0 %copy-start = (bf16[768,64]{0,1:T(8,128)(2,1)S(1)}, bf16[768,64]{0,1:T(8,128)(2,1)}, u32[]{:S(2)}) copy-start(bf16[768,64]{0,1:T(8,128)(2,1)} %param.7) | copy-start | bytes 294916
  7.2 68.8 %copy-start.1 = (f32[512]{0:T(512)S(1)}, f32[512]{0:T(512)}, u32[]{:S(2)}) copy-start(f32[512]{0:T(512)} %param.6) | copy-start | bytes 6148
  7.2 68.8 %all-reduce.2.cloned.1.call-start = ((), (), s32[]{:S(2)}) async-start(), calls=%async_computation.1 | async-start | bytes 3145728 | tf_op jit(solution)/shard_map/psum | solution.py:15
  22.1 223.1 %reduce-scatter.2.cloned.1.call-start = ((), (), s32[]{:S(2)}) async-start(), calls=%async_computation.2 | async-start | bytes 1351680 | tf_op jit(solution)/shard_map/reduce_scatter | solution.py:18
Sparse Core Ops, SparseCore 0:
  22.2 53.7 all-reduce.1
  84.2 160.9 reduce-scatter.1
where the time goes:
time: 255 us
  waiting for transfers between devices  215 us (84%)
  matrix products  16.7 us (7%)
  between operations  14.1 us (6%)
  other arithmetic  8.86 us (3%)
    reduce_scatter x1, waiting for transfers between devices, on_device(): lax.psum_scatter(lax.dot_general(features, right_side, (((0,), (0,)), (()...  161 us
    psum x1, waiting for transfers between devices, on_device(): projection = lax.psum(partial_value, 'marker')  53.7 us
    dot_general x1, matrix products, on_device(): jnp.dot(dosage, frequencies, preferred_element_type=jnp.float32)  14.9 us
    convert_element_type x1, other arithmetic, on_device(): (math.sqrt(2.0) * jnp.cos(projection + phases)).astype(jnp.bfloat16)  6.19 us
  transfers between devices with their start and end apart: 2, of which 2 were waited for; matrix products, arithmetic and copies ran while one was open for 0% of the time, Pallas kernels for 0%

commit v1 on v0

v1 whole, which is shorter than its diff:
```python
import functools
import math

import jax
import jax.numpy as jnp
from jax import lax
from jax.experimental import pallas as pl
from jax.experimental.pallas import tpu as pltpu
from jax.sharding import PartitionSpec as P

OTHER_CORE = [(0, 1), (1, 0), (2, 3), (3, 2)]
OTHER_CHIP = [(0, 2), (2, 0), (1, 3), (3, 1)]
STEP = 1024
SINE = (-8.88576566829991, 58.46592923637672, -115.4012466635561, 108.25774031408996, -55.913345915340486)


def to_turns(radians):
    steps = jnp.round(radians * (65536.0 / (2.0 * math.pi))).astype(jnp.int32)
    return ((steps << 16) >> 16).astype(jnp.int16)


def accumulate(geno, panel, acc):
    dosage = (geno - 1).astype(jnp.float32).astype(jnp.bfloat16)
    acc[...] += jnp.dot(dosage, panel, preferred_element_type=jnp.float32)


def first_half_kernel(geno_hbm, panel_hbm, out_ref, panel_ref, geno_buf, acc, geno_sem, panel_sem):
    rows = acc.shape[0]
    steps = geno_buf.shape[0]
    first = pl.multiple_of((1 - lax.axis_index("marker") % 2) * rows, rows)

    def panel_copy(k):
        part = pl.ds(pl.multiple_of(k * STEP, STEP), STEP)
        return pltpu.make_async_copy(panel_hbm.at[part], panel_ref.at[part], panel_sem.at[k])

    def geno_copy(k):
        part = pl.ds(pl.multiple_of(k * STEP, STEP), STEP)
        return pltpu.make_async_copy(geno_hbm.at[pl.ds(first, rows), part], geno_buf.at[k], geno_sem.at[k])

    for k in range(steps):
        panel_copy(k).start()
        geno_copy(k).start()
    acc[...] = jnp.zeros_like(acc)

    @pl.loop(0, steps)
    def _(k):
        panel_copy(k).wait()
        geno_copy(k).wait()
        accumulate(geno_buf[k], panel_ref[pl.ds(pl.multiple_of(k * STEP, STEP), STEP)], acc)

    out_ref[...] = to_turns(acc[...])


def second_half_kernel(geno_hbm, panel_ref, out_ref, geno_buf, acc, geno_sem):
    rows = acc.shape[0]
    steps = geno_buf.shape[0]
    first = pl.multiple_of((lax.axis_index("marker") % 2) * rows, rows)

    def geno_copy(k):
        part = pl.ds(pl.multiple_of(k * STEP, STEP), STEP)
        return pltpu.make_async_copy(geno_hbm.at[pl.ds(first, rows), part], geno_buf.at[k], geno_sem.at[k])

    for k in range(steps):
        geno_copy(k).start()
    acc[...] = jnp.zeros_like(acc)

    @pl.loop(0, steps)
    def _(k):
        geno_copy(k).wait()
        accumulate(geno_buf[k], panel_ref[pl.ds(pl.multiple_of(k * STEP, STEP), STEP)], acc)

    out_ref[...] = to_turns(acc[...])


def features_kernel(here_ref, there_ref, phase_ref, out_ref):
    turns = here_ref[...].astype(jnp.int32) + there_ref[...].astype(jnp.int32)
    turns = ((turns << 16) >> 16).astype(jnp.float32) * (1.0 / 65536.0)
    turns = turns + phase_ref[...] * (1.0 / (2.0 * math.pi))
    turns = turns - jnp.round(turns)
    t = jnp.abs(turns) - 0.25
    square = t * t
    value = jnp.full_like(t, SINE[-1])
    for factor in SINE[-2::-1]:
        value = value * square + factor
    out_ref[...] = (value * t).astype(jnp.bfloat16)


def gram_kernel(own_ref, other_ref, pheno_ref, out_ref):
    rows, feats = own_ref.shape
    half = feats // 2
    core = lax.axis_index("marker") % 2
    cols = pl.ds(pl.multiple_of(core * half, half), half)
    contract = (((0,), (0,)), ((), ()))

    def product(left, right):
        return lax.dot_general(left, right, contract, preferred_element_type=jnp.float32)

    own_pheno = pheno_ref[pl.ds(pl.multiple_of(core * rows, rows), rows)]
    other_pheno = pheno_ref[pl.ds(pl.multiple_of((1 - core) * rows, rows), rows)]
    gram = product(own_ref[...], own_ref[:, cols]) + product(other_ref[...], other_ref[:, cols])
    cross = product(own_ref[...], own_pheno) + product(other_ref[...], other_pheno)
    high = cross.astype(jnp.bfloat16)
    low = (cross - high.astype(jnp.float32)).astype(jnp.bfloat16)
    out_ref[:, :half] = gram.astype(jnp.bfloat16)
    out_ref[:, half:] = jnp.where(core == 0, high, low)


def sum_kernel(parts, in_ref, out_ref):
    wide = in_ref[...].astype(jnp.float32)
    out_ref[...] = jnp.sum(wide.reshape(parts, wide.shape[0] // parts, wide.shape[1]), axis=0)


def finish_kernel(animals_all, own_ref, other_ref, gram_ref, cross_ref):
    half = gram_ref.shape[1] // 2
    core = lax.axis_index("marker") % 2
    here = pl.ds(pl.multiple_of(core * half, half), half)
    there = pl.ds(pl.multiple_of((1 - core) * half, half), half)
    gram_ref[:, here] = own_ref[:, :half] / animals_all
    gram_ref[:, there] = other_ref[:, :half] / animals_all
    cross_ref[...] = (own_ref[:, half:] + other_ref[:, half:]) / math.sqrt(animals_all)


def vmem():
    return pl.BlockSpec(memory_space=pltpu.VMEM)


def anywhere():
    return pl.BlockSpec(memory_space=pl.ANY)


def on_device(genotypes, frequencies, phases, phenotypes):
    rows, markers = genotypes.shape
    feats = frequencies.shape[1]
    traits = phenotypes.shape[1]
    groups = lax.axis_size("animal")
    animals_all = float(groups * rows)
    half = rows // 2
    steps = markers // STEP
    scratch = [
        pltpu.VMEM((steps, half, STEP), jnp.int32),
        pltpu.VMEM((half, feats), jnp.float32),
        pltpu.SemaphoreType.DMA((steps,)),
    ]
    flops = 2 * half * markers * feats
    params = pltpu.CompilerParams(vmem_limit_bytes=24 * 2**20)
    small = pltpu.CompilerParams(vmem_limit_bytes=12 * 2**20)

    with jax.named_scope("projection_other_rows"):
        to_send, panel = pl.pallas_call(
            first_half_kernel,
            out_shape=(jax.ShapeDtypeStruct((half, feats), jnp.int16), pltpu.VMEM((markers, feats), jnp.bfloat16)),
            in_specs=[anywhere(), anywhere()],
            out_specs=(vmem(), vmem()),
            scratch_shapes=scratch + [pltpu.SemaphoreType.DMA((steps,))],
            compiler_params=params,
            cost_estimate=pl.CostEstimate(flops=flops, bytes_accessed=half * markers * 4 + markers * feats * 2, transcendentals=0),
        )(genotypes, frequencies)
    received = lax.ppermute(to_send, "marker", OTHER_CORE)
    with jax.named_scope("projection_own_rows"):
        kept = pl.pallas_call(
            second_half_kernel,
            out_shape=jax.ShapeDtypeStruct((half, feats), jnp.int16),
            in_specs=[anywhere(), vmem()],
            out_specs=vmem(),
            scratch_shapes=scratch,
            compiler_params=params,
            cost_estimate=pl.CostEstimate(flops=flops, bytes_accessed=half * markers * 4, transcendentals=0),
        )(genotypes, panel)
    chip_sum = kept + received
    chip_other = lax.ppermute(chip_sum, "marker", OTHER_CHIP)
    with jax.named_scope("features"):
        features = pl.pallas_call(
            features_kernel,
            out_shape=jax.ShapeDtypeStruct((half, feats), jnp.bfloat16),
            in_specs=[vmem()] * 3,
            out_specs=vmem(),
            compiler_params=small,
        )(chip_sum, chip_other, phases.reshape(1, feats))
    features_other = lax.ppermute(features, "marker", OTHER_CORE)
    with jax.named_scope("gram_cross"):
        partial_sums = pl.pallas_call(
            gram_kernel,
            out_shape=jax.ShapeDtypeStruct((feats, feats // 2 + traits), jnp.bfloat16),
            in_specs=[vmem()] * 3,
            out_specs=vmem(),
            compiler_params=small,
        )(features, features_other, phenotypes)
    pieces = lax.all_to_all(partial_sums, "animal", 0, 0, tiled=True)
    with jax.named_scope("sum_animals"):
        own = pl.pallas_call(
            functools.partial(sum_kernel, groups),
            out_shape=jax.ShapeDtypeStruct((feats // groups, feats // 2 + traits), jnp.float32),
            in_specs=[vmem()],
            out_specs=vmem(),
            compiler_params=small,
        )(pieces)
    other = lax.ppermute(own, "marker", OTHER_CORE)
    with jax.named_scope("finish"):
        return pl.pallas_call(
            functools.partial(finish_kernel, animals_all),
            out_shape=(
                jax.ShapeDtypeStruct((feats // groups, feats), jnp.float32),
                jax.ShapeDtypeStruct((feats // groups, traits), jnp.float32),
            ),
            in_specs=[vmem()] * 2,
            out_specs=(vmem(), vmem()),
            compiler_params=small,
        )(own, other)


def solution(mesh):
    in_specs = (P("animal", "marker"), P("marker", None), P(), P("animal", None))
    out_specs = (P("animal", None), P("animal", None))
    return jax.shard_map(
        on_device, mesh=mesh, in_specs=in_specs, out_specs=out_specs, check_vma=False
    )
```

time: 255 us -> 55.9 us (0.22)
  the two profiles are of different devices: /device:TPU:0 before, /device:TPU:1 now
where the time goes in v1:
time: 55.9 us; the launch traced here: 55.7 us
  blocking collectives  17.2 us (31%)
  Pallas kernels  14.6 us (26%)
  waiting for transfers between devices  11.5 us (21%)
  starting transfers between devices  8.01 us (14%)
  local copies, waits for them, and re-layouts  3.54 us (6%)
  between operations  0.69 us (1%)
    all_to_all x1, blocking collectives, on_device(): pieces = lax.all_to_all(partial_sums, 'animal', 0, 0, tiled=True)  17.2 us
    ppermute x1, waiting for transfers between devices, on_device(): chip_other = lax.ppermute(chip_sum, 'marker', OTHER_CHIP)  9.47 us
    pallas_call x1, Pallas kernels, on_device(): pl.pallas_call(first_half_kernel, out_shape=(jax.ShapeDtypeStruct((half,...  6.38 us
    pallas_call x1, Pallas kernels, on_device(): pl.pallas_call(second_half_kernel, out_shape=jax.ShapeDtypeStruct((half,...  6.3 us
    ppermute x1, starting transfers between devices, on_device(): chip_other = lax.ppermute(chip_sum, 'marker', OTHER_CHIP)  3.75 us
    unnamed x7, local copies, waits for them, and re-layouts  3.54 us
    ppermute x1, starting transfers between devices, on_device(): other = lax.ppermute(own, 'marker', OTHER_CORE)  2.06 us
    ppermute x1, starting transfers between devices, on_device(): received = lax.ppermute(to_send, 'marker', OTHER_CORE)  1.51 us
  transfers between devices with their start and end apart: 4, of which 3 were waited for; matrix products, arithmetic and copies ran while one was open for 0% of the time, Pallas kernels for 11%

profile of v1, /device:TPU:1, one launch (start us, length us, event | category | flops | bytes accessed | tf_op | source)
XLA Modules:
  0.0 55.7 jit_solution(3164649760436692879)
XLA Ops:
  0.6 0.0 copy-start
  0.6 3.4 %copy-done = bf16[8192,512]{1,0:T(8,128)(2,1)S(1)} copy-done((bf16[8192,512]{1,0:T(8,128)(2,1)S(1)}, bf16[8192,512]{1,0:T(8,128)(2,1)}, u32[]{:S(2)}) %copy-start) | copy-done | bytes 8388632
  4.0 6.4 %projection_other_rows.1 = (s16[384,512]{1,0:T(8,128)(2,1)S(1)}, bf16[8192,512]{1,0:T(8,128)(2,1)S(1)}) custom-call(s32[768,8192]{1,0:T(8,128)} %geno_hbm.3, bf16[8192,512]{1,0:T(8,128)(2,1)S(1)} %copy-done), custom_call_target="tpu_custom_call" | custom-call | flops 3221225472 | bytes 20971520 | tf_op jit(solution)/shard_map/projection_other_rows/pallas_call | solution.py:149
  10.4 1.5 %collective-permute-start = (s16[384,512]{1,0:T(8,128)(2,1)S(1)}, s16[384,512]{1,0:T(8,128)(2,1)S(1)}, u32[]{:S(2)}, u32[]{:S(2)}) collective-permute-start(s16[384,512]{1,0:T(8,128)(2,1)S(1)} %get-tuple-element.5), channel_id=1, source_target_pairs={{0,32},{32,0},{64,96},{96,64},{1,33},{33,1},{65,97},{97,65},{2,34}... | collective-permute-start | bytes 1179656 | tf_op jit(solution)/shard_map/ppermute | solution.py:158
  11.9 0.0 copy-start.1
  11.9 0.0 copy-start.2
  11.9 6.3 %projection_own_rows.1 = s16[384,512]{1,0:T(8,128)(2,1)S(1)} custom-call(s32[768,8192]{1,0:T(8,128)} %geno_hbm.3, bf16[8192,512]{1,0:T(8,128)(2,1)S(1)} %get-tuple-element.4.panel_ref), custom_call_target="tpu_custom_call" | custom-call | flops 3221225472 | bytes 12582912 | tf_op jit(solution)/shard_map/projection_own_rows/pallas_call | solution.py:160
  18.2 0.0 collective-permute-done
  18.2 0.1 add.3.here_ref
  18.3 3.8 %collective-permute-start.1 = (s16[384,512]{1,0:T(8,128)(2,1)S(1)}, s16[384,512]{1,0:T(8,128)(2,1)S(1)}, u32[]{:S(2)}, u32[]{:S(2)}) collective-permute-start(s16[384,512]{1,0:T(8,128)(2,1)S(1)} %add.3.here_ref), channel_id=1, source_target_pairs={{0,64},{64,0},{32,96},{96,32},{1,65},{65,1},{33,97},{97,33},{2,66}... | collective-permute-start | bytes 1179656 | tf_op jit(solution)/shard_map/ppermute | solution.py:170
  22.1 9.5 %collective-permute-done.1.there_ref = s16[384,512]{1,0:T(8,128)(2,1)S(1)} collective-permute-done((s16[384,512]{1,0:T(8,128)(2,1)S(1)}, s16[384,512]{1,0:T(8,128)(2,1)S(1)}, u32[]{:S(2)}, u32[]{:S(2)}) %collective-permute-start.1) | collective-permute-done | bytes 393248 | tf_op jit(solution)/shard_map/ppermute | solution.py:170
  31.6 0.0 copy-done.1
  31.6 0.6 %features.1.own_ref = bf16[384,512]{1,0:T(8,128)(2,1)S(1)} custom-call(s16[384,512]{1,0:T(8,128)(2,1)S(1)} %add.3.here_ref, s16[384,512]{1,0:T(8,128)(2,1)S(1)} %collective-permute-done.1.there_ref, f32[1,512]{1,0:T(1,128)S(1)} %bitcast.5), custom_call_target="tpu_custom_call" | custom-call | tf_op jit(solution)/shard_map/features/pallas_call | solution.py:172
  32.1 0.7 %collective-permute-start.2 = (bf16[384,512]{1,0:T(8,128)(2,1)S(1)}, bf16[384,512]{1,0:T(8,128)(2,1)S(1)}, u32[]{:S(2)}, u32[]{:S(2)}) collective-permute-start(bf16[384,512]{1,0:T(8,128)(2,1)S(1)} %features.1.own_ref), channel_id=1, source_target_pairs={{0,32},{32,0},{64,96},{96,64},{1,33},{33,1},{65,97},{97,65},{2,34}... | collective-permute-start | bytes 1179656 | tf_op jit(solution)/shard_map/ppermute | solution.py:179
  32.8 0.0 copy-done.2
  32.8 0.2 copy.6.pheno_ref
  33.0 1.2 %collective-permute-done.2.other_ref = bf16[384,512]{1,0:T(8,128)(2,1)S(1)} collective-permute-done((bf16[384,512]{1,0:T(8,128)(2,1)S(1)}, bf16[384,512]{1,0:T(8,128)(2,1)S(1)}, u32[]{:S(2)}, u32[]{:S(2)}) %collective-permute-start.2) | collective-permute-done | bytes 393248 | tf_op jit(solution)/shard_map/ppermute | solution.py:179
  34.2 0.7 %gram_cross.1 = bf16[512,320]{1,0:T(8,128)(2,1)S(1)} custom-call(bf16[384,512]{1,0:T(8,128)(2,1)S(1)} %features.1.own_ref, bf16[384,512]{1,0:T(8,128)(2,1)S(1)} %collective-permute-done.2.other_ref, bf16[768,64]{1,0:T(8,128)(2,1)S(1)} %copy.6.pheno_ref), custom_call_target="tpu_custom_call" | custom-call | tf_op jit(solution)/shard_map/gram_cross/pallas_call | solution.py:181
  34.9 17.2 %all_to_all.11 = bf16[32,16,320]{2,1,0:T(8,128)(2,1)S(1)} all-to-all(bf16[32,16,320]{2,1,0:T(8,128)(2,1)S(1)} %bitcast.4), channel_id=1, replica_groups=mesh['marker'=4,'animal'=32] {'animal'}, dimensions={0} | all-to-all | bytes 655360 | tf_op jit(solution)/shard_map/all_to_all | solution.py:188
  52.1 0.1 sum_animals.1.own_ref
  52.2 2.1 %collective-permute-start.3 = (f32[16,320]{1,0:T(8,128)S(1)}, f32[16,320]{1,0:T(8,128)S(1)}, u32[]{:S(2)}, u32[]{:S(2)}) collective-permute-start(f32[16,320]{1,0:T(8,128)S(1)} %sum_animals.1.own_ref), channel_id=1, source_target_pairs={{0,32},{32,0},{64,96},{96,64},{1,33},{33,1},{65,97},{97,65},{2,34}... | collective-permute-start | bytes 61448 | tf_op jit(solution)/shard_map/ppermute | solution.py:197
  54.2 0.8 %collective-permute-done.3.other_ref = f32[16,320]{1,0:T(8,128)S(1)} collective-permute-done((f32[16,320]{1,0:T(8,128)S(1)}, f32[16,320]{1,0:T(8,128)S(1)}, u32[]{:S(2)}, u32[]{:S(2)}) %collective-permute-start.3) | collective-permute-done | bytes 20512 | tf_op jit(solution)/shard_map/ppermute | solution.py:197
  55.1 0.6 %finish.1 = (f32[16,512]{1,0:T(8,128)}, f32[16,64]{1,0:T(8,128)}) custom-call(f32[16,320]{1,0:T(8,128)S(1)} %sum_animals.1.own_ref, f32[16,320]{1,0:T(8,128)S(1)} %collective-permute-done.3.other_ref), custom_call_target="tpu_custom_call" | custom-call | tf_op jit(solution)/shard_map/finish/pallas_call | solution.py:199
Async XLA Ops:
  0.6 3.4 %copy-start = (bf16[8192,512]{1,0:T(8,128)(2,1)S(1)}, bf16[8192,512]{1,0:T(8,128)(2,1)}, u32[]{:S(2)}) copy-start(bf16[8192,512]{1,0:T(8,128)(2,1)} %panel_hbm.1) | copy-start | bytes 25165828
  10.4 7.8 %collective-permute-start = (s16[384,512]{1,0:T(8,128)(2,1)S(1)}, s16[384,512]{1,0:T(8,128)(2,1)S(1)}, u32[]{:S(2)}, u32[]{:S(2)}) collective-permute-start(s16[384,512]{1,0:T(8,128)(2,1)S(1)} %get-tuple-element.5), channel_id=1, source_target_pairs={{0,32},{32,0},{64,96},{96,64},{1,33},{33,1},{65,97},{97,65},{2,34}... | collective-permute-start | bytes 1179656 | tf_op jit(solution)/shard_map/ppermute | solution.py:158
  11.9 19.6 %copy-start.1 = (f32[512]{0:T(512)S(1)}, f32[512]{0:T(512)}, u32[]{:S(2)}) copy-start(f32[512]{0:T(512)} %param.6) | copy-start | bytes 6148
  11.9 20.9 %copy-start.2 = (bf16[768,64]{0,1:T(8,128)(2,1)S(1)}, bf16[768,64]{0,1:T(8,128)(2,1)}, u32[]{:S(2)}) copy-start(bf16[768,64]{0,1:T(8,128)(2,1)} %param.7) | copy-start | bytes 294916
  18.3 13.2 %collective-permute-start.1 = (s16[384,512]{1,0:T(8,128)(2,1)S(1)}, s16[384,512]{1,0:T(8,128)(2,1)S(1)}, u32[]{:S(2)}, u32[]{:S(2)}) collective-permute-start(s16[384,512]{1,0:T(8,128)(2,1)S(1)} %add.3.here_ref), channel_id=1, source_target_pairs={{0,64},{64,0},{32,96},{96,32},{1,65},{65,1},{33,97},{97,33},{2,66}... | collective-permute-start | bytes 1179656 | tf_op jit(solution)/shard_map/ppermute | solution.py:170
  32.1 2.0 %collective-permute-start.2 = (bf16[384,512]{1,0:T(8,128)(2,1)S(1)}, bf16[384,512]{1,0:T(8,128)(2,1)S(1)}, u32[]{:S(2)}, u32[]{:S(2)}) collective-permute-start(bf16[384,512]{1,0:T(8,128)(2,1)S(1)} %features.1.own_ref), channel_id=1, source_target_pairs={{0,32},{32,0},{64,96},{96,64},{1,33},{33,1},{65,97},{97,65},{2,34}... | collective-permute-start | bytes 1179656 | tf_op jit(solution)/shard_map/ppermute | solution.py:179
  52.2 2.9 %collective-permute-start.3 = (f32[16,320]{1,0:T(8,128)S(1)}, f32[16,320]{1,0:T(8,128)S(1)}, u32[]{:S(2)}, u32[]{:S(2)}) collective-permute-start(f32[16,320]{1,0:T(8,128)S(1)} %sum_animals.1.own_ref), channel_id=1, source_target_pairs={{0,32},{32,0},{64,96},{96,64},{1,33},{33,1},{65,97},{97,65},{2,34}... | collective-permute-start | bytes 61448 | tf_op jit(solution)/shard_map/ppermute | solution.py:197

commit v2 on v1

v2 whole, which is shorter than its diff:
```python
import functools
import math

import jax
import jax.numpy as jnp
from jax import lax
from jax.experimental import pallas as pl
from jax.experimental.pallas import tpu as pltpu
from jax.sharding import PartitionSpec as P

OTHER_CORE = [(0, 1), (1, 0), (2, 3), (3, 2)]
OTHER_CHIP = [(0, 2), (2, 0), (1, 3), (3, 1)]
OTHER_BOTH = [(0, 3), (3, 0), (1, 2), (2, 1)]
TILE = 256
PARTS = [(0, 512)] + [(512 + 1024 * k, 1024) for k in range(7)] + [(7680, 512)]
SINE = (-8.88576566829991, 58.46592923637672, -115.4012466635561, 108.25774031408996, -55.913345915340486)


def to_turns(radians):
    steps = jnp.round(radians * (65536.0 / (2.0 * math.pi))).astype(jnp.int32)
    return ((steps << 16) >> 16).astype(jnp.int16)


def project(geno, panel, before, put):
    def run(*sums):
        for step, (start, width) in enumerate(PARTS):
            before(step)
            for tile in range(start, start + width, TILE):
                dosage = (geno[:, tile : tile + TILE] - 1).astype(jnp.float32).astype(jnp.bfloat16)
                slot = tile // TILE % 2
                for unit in range(2):
                    pltpu.matmul_push_rhs(panel[tile : tile + TILE, unit * TILE : (unit + 1) * TILE], slot, unit)
                for unit in range(2):
                    pltpu.matmul_acc_lhs(sums[unit], dosage, slot)
        for unit in range(2):
            put(to_turns(pltpu.matmul_pop(sums[unit])), slice(unit * TILE, (unit + 1) * TILE))

    pl.run_scoped(run, *[pltpu.ACC(unit)((geno.shape[0], TILE), jnp.float32) for unit in range(2)])


def copies(geno_hbm, group, geno, sem):
    rows = geno.shape[0] // 2
    core = lax.axis_index("marker") % 2
    firsts = (pl.multiple_of((group * 2 + 1 - core) * rows, rows), pl.multiple_of((group * 2 + core) * rows, rows))
    return [
        [
            pltpu.make_async_copy(
                geno_hbm.at[pl.ds(first, rows), pl.ds(start, width)],
                geno.at[pl.ds(place * rows, rows), pl.ds(start, width)],
                sem.at[step, place],
            )
            for place, first in enumerate(firsts)
        ]
        for step, (start, width) in enumerate(PARTS)
    ]


def store(send_ref, keep_ref):
    rows = send_ref.shape[0]

    def put(turns, cols):
        send_ref[:, cols] = turns[:rows]
        keep_ref[:, cols] = turns[rows:]

    return put


def first_kernel(geno_hbm, panel_hbm, send_ref, keep_ref, panel_ref, geno, geno_sem, panel_sem):
    chip = lax.axis_index("marker") // 2
    geno_copies = copies(geno_hbm, 1 - chip, geno, geno_sem)
    panel_copies = [
        pltpu.make_async_copy(panel_hbm.at[pl.ds(start, width)], panel_ref.at[pl.ds(start, width)], panel_sem.at[step])
        for step, (start, width) in enumerate(PARTS)
    ]
    for panel_copy, pair in zip(panel_copies, geno_copies):
        for copy in [panel_copy] + pair:
            copy.start()

    def before(step):
        for copy in [panel_copies[step]] + geno_copies[step]:
            copy.wait()

    project(geno, panel_ref, before, store(send_ref, keep_ref))


def second_kernel(geno_hbm, panel_ref, _, send_ref, keep_ref, geno, geno_sem):
    geno_copies = copies(geno_hbm, lax.axis_index("marker") // 2, geno, geno_sem)
    for pair in geno_copies:
        for copy in pair:
            copy.start()

    def before(step):
        for copy in geno_copies[step]:
            copy.wait()

    project(geno, panel_ref, before, store(send_ref, keep_ref))


def features_kernel(kept_ref, core_ref, phase_ref, out_ref):
    turns = kept_ref[...].astype(jnp.int32) + core_ref[...].astype(jnp.int32)
    turns = ((turns << 16) >> 16).astype(jnp.float32) * (1.0 / 65536.0)
    turns = turns + phase_ref[...] * (1.0 / (2.0 * math.pi))
    turns = turns - jnp.round(turns)
    t = jnp.abs(turns) - 0.25
    square = t * t
    value = jnp.full_like(t, SINE[-1])
    for factor in SINE[-2::-1]:
        value = value * square + factor
    out_ref[...] = (value * t).astype(jnp.bfloat16)


def gram_kernel(own_ref, other_ref, pheno_ref, out_ref):
    rows, feats = own_ref.shape
    half = feats // 2
    place = lax.axis_index("marker")
    core = place % 2
    cols = pl.ds(pl.multiple_of(core * half, half), half)
    blocks = [(own_ref, place), (other_ref, place + 1 - 2 * core)]

    def product(left, right):
        return lax.dot_general(left, right, (((0,), (0,)), ((), ())), preferred_element_type=jnp.float32)

    gram = sum(product(ref[...], ref[:, cols]) for ref, _ in blocks)
    cross = sum(product(ref[...], pheno_ref[pl.ds(pl.multiple_of(spot * rows, rows), rows)]) for ref, spot in blocks)
    high = cross.astype(jnp.bfloat16)
    low = (cross - high.astype(jnp.float32)).astype(jnp.bfloat16)
    out_ref[:, :half] = gram.astype(jnp.bfloat16)
    out_ref[:, half:] = jnp.where(core == 0, high, low)


def sum_kernel(parts, in_ref, out_ref):
    wide = in_ref[...].astype(jnp.float32)
    out_ref[...] = jnp.sum(wide.reshape(parts, wide.shape[0] // parts, wide.shape[1]), axis=0)


def finish_kernel(animals_all, own_ref, core_ref, chip_ref, both_ref, gram_ref, cross_ref):
    half = gram_ref.shape[1] // 2
    core = lax.axis_index("marker") % 2
    here = pl.ds(pl.multiple_of(core * half, half), half)
    there = pl.ds(pl.multiple_of((1 - core) * half, half), half)
    own = own_ref[...] + chip_ref[...]
    other = core_ref[...] + both_ref[...]
    gram_ref[:, here] = own[:, :half] / animals_all
    gram_ref[:, there] = other[:, :half] / animals_all
    cross_ref[...] = (own[:, half:] + other[:, half:]) / math.sqrt(animals_all)


def vmem():
    return pl.BlockSpec(memory_space=pltpu.VMEM)


def anywhere():
    return pl.BlockSpec(memory_space=pl.ANY)


def on_device(genotypes, frequencies, phases, phenotypes):
    rows, markers = genotypes.shape
    feats = frequencies.shape[1]
    traits = phenotypes.shape[1]
    groups = lax.axis_size("animal")
    animals_all = float(groups * rows)
    half, quarter = rows // 2, rows // 4
    small = pltpu.CompilerParams(vmem_limit_bytes=12 * 2**20)
    dma = pltpu.SemaphoreType.DMA
    genotypes = pltpu.with_memory_space_constraint(genotypes, pltpu.HBM)
    frequencies = pltpu.with_memory_space_constraint(frequencies, pltpu.HBM)

    def cost(height, more=0):
        return pl.CostEstimate(flops=2 * height * markers * feats, bytes_accessed=height * markers * 4 + more, transcendentals=0)

    part = jax.ShapeDtypeStruct((quarter, feats), jnp.int16)
    geno_scratch = [pltpu.VMEM((half, markers), jnp.int32), dma((len(PARTS), 2))]
    params = pltpu.CompilerParams(vmem_limit_bytes=20 * 2**20)
    with jax.named_scope("projection_other_chip"):
        to_core, kept, panel = pl.pallas_call(
            first_kernel,
            out_shape=(part, part, pltpu.VMEM((markers, feats), jnp.bfloat16)),
            in_specs=[anywhere(), anywhere()],
            out_specs=(vmem(), vmem(), vmem()),
            scratch_shapes=geno_scratch + [dma((len(PARTS),))],
            compiler_params=params,
            cost_estimate=cost(half, markers * feats * 2),
        )(genotypes, frequencies)
    to_chip = kept + lax.ppermute(to_core, "marker", OTHER_CORE)
    from_chip = lax.ppermute(to_chip, "marker", OTHER_CHIP)
    with jax.named_scope("projection_this_chip"):
        to_core, kept = pl.pallas_call(
            second_kernel,
            out_shape=(part, part),
            in_specs=[anywhere(), vmem(), anywhere()],
            out_specs=(vmem(), vmem()),
            scratch_shapes=geno_scratch,
            compiler_params=params,
            cost_estimate=cost(half),
        )(genotypes, panel, to_chip)
    from_core = lax.ppermute(to_core, "marker", OTHER_CORE)
    with jax.named_scope("features"):
        features = pl.pallas_call(
            features_kernel,
            out_shape=jax.ShapeDtypeStruct((quarter, feats), jnp.bfloat16),
            in_specs=[vmem()] * 3,
            out_specs=vmem(),
            compiler_params=small,
        )(kept + from_chip, from_core, phases.reshape(1, feats))
    features_other = lax.ppermute(features, "marker", OTHER_CORE)
    with jax.named_scope("gram_cross"):
        partial_sums = pl.pallas_call(
            gram_kernel,
            out_shape=jax.ShapeDtypeStruct((feats, feats // 2 + traits), jnp.bfloat16),
            in_specs=[vmem()] * 3,
            out_specs=vmem(),
            compiler_params=small,
        )(features, features_other, phenotypes)
    pieces = lax.all_to_all(partial_sums, "animal", 0, 0, tiled=True)
    with jax.named_scope("sum_animals"):
        own = pl.pallas_call(
            functools.partial(sum_kernel, groups),
            out_shape=jax.ShapeDtypeStruct((feats // groups, feats // 2 + traits), jnp.float32),
            in_specs=[vmem()],
            out_specs=vmem(),
            compiler_params=small,
        )(pieces)
    others = [lax.ppermute(own, "marker", pairs) for pairs in (OTHER_CORE, OTHER_CHIP, OTHER_BOTH)]
    with jax.named_scope("finish"):
        return pl.pallas_call(
            functools.partial(finish_kernel, animals_all),
            out_shape=(
                jax.ShapeDtypeStruct((feats // groups, feats), jnp.float32),
                jax.ShapeDtypeStruct((feats // groups, traits), jnp.float32),
            ),
            in_specs=[vmem()] * 4,
            out_specs=(vmem(), vmem()),
            compiler_params=small,
        )(own, *others)


def solution(mesh):
    in_specs = (P("animal", "marker"), P("marker", None), P(), P("animal", None))
    out_specs = (P("animal", None), P("animal", None))
    return jax.shard_map(
        on_device, mesh=mesh, in_specs=in_specs, out_specs=out_specs, check_vma=False
    )
```

time: 55.9 us -> 50.9 us (0.911)
  waiting for transfers between devices: 11.5 us -> 6.3 us
  starting transfers between devices: 8.01 us -> 11.7 us
  local copies, waits for them, and re-layouts: 3.54 us -> 0.17 us
    ppermute x3 -> x6, waiting for transfers between devices: 10.3 us -> 5.4 us  [the longest x3 3.31 us: on_device(): lax.ppermute(own, 'marker', pairs)]
    ppermute x3 -> x6, starting transfers between devices: 7.33 us -> 11.3 us  [the longest x3 5.29 us: on_device(): lax.ppermute(own, 'marker', pairs)]
    unnamed x7 -> x5, local copies, waits for them, and re-layouts: 3.54 us -> 0.17 us
  transfers between devices with their start and end apart: 4 -> 7, of which waited for: 3 -> 5; matrix products, arithmetic and copies ran while one was open for 0% -> 0% of each run, Pallas kernels for 11% -> 11%
where the time goes in v2:
time: 50.9 us; the launch traced here: 50.7 us
  blocking collectives  16.9 us (33%)
  Pallas kernels  14.8 us (29%)
  starting transfers between devices  11.7 us (23%)
  waiting for transfers between devices  6.3 us (12%)
  between operations  0.68 us (1%)
    all_to_all x1, blocking collectives, on_device(): pieces = lax.all_to_all(partial_sums, 'animal', 0, 0, tiled=True)  16.9 us
    pallas_call x1, Pallas kernels, on_device(): pl.pallas_call(first_kernel, out_shape=(part, part, pltpu.VMEM((markers,...  7.79 us
    pallas_call x1, Pallas kernels, on_device(): pl.pallas_call(second_kernel, out_shape=(part, part), in_specs=[anywhere(...  5.54 us
    ppermute x3, starting transfers between devices, on_device(): lax.ppermute(own, 'marker', pairs)  5.29 us
    ppermute x1, starting transfers between devices, on_device(): from_chip = lax.ppermute(to_chip, 'marker', OTHER_CHIP)  3.76 us
    ppermute x3, waiting for transfers between devices, on_device(): lax.ppermute(own, 'marker', pairs)  3.31 us
    ppermute x1, starting transfers between devices, on_device(): to_chip = kept + lax.ppermute(to_core, 'marker', OTHER_CORE)  1.5 us
    ppermute x1, waiting for transfers between devices, on_device(): to_chip = kept + lax.ppermute(to_core, 'marker', OTHER_CORE)  1.07 us
  transfers between devices with their start and end apart: 7, of which 5 were waited for; matrix products, arithmetic and copies ran while one was open for 0% of the time, Pallas kernels for 11%

profile of v2, /device:TPU:1, one launch (start us, length us, event | category | flops | bytes accessed | tf_op | source)
XLA Modules:
  0.0 50.7 jit_solution(4744532869039565659)
XLA Ops:
  0.6 7.8 %projection_other_chip.1 = (s16[192,512]{1,0:T(8,128)(2,1)S(1)}, s16[192,512]{1,0:T(8,128)(2,1)S(1)}, bf16[8192,512]{1,0:T(8,128)(2,1)S(1)}) custom-call(s32[768,8192]{1,0:T(8,128)} %geno_hbm.3, bf16[8192,512]{1,0:T(8,128)(2,1)} %panel_hbm.1), custom_call_target="tpu_custom_call" | custom-call | flops 3221225472 | bytes 20971520 | tf_op jit(solution)/shard_map/projection_other_chip/pallas_call | solution.py:175
  8.4 1.5 %collective-permute-start = (s16[192,512]{1,0:T(8,128)(2,1)S(1)}, s16[192,512]{1,0:T(8,128)(2,1)S(1)}, u32[]{:S(2)}, u32[]{:S(2)}) collective-permute-start(s16[192,512]{1,0:T(8,128)(2,1)S(1)} %get-tuple-element.9), channel_id=1, source_target_pairs={{0,32},{32,0},{64,96},{96,64},{1,33},{33,1},{65,97},{97,65},{2,34}... | collective-permute-start | bytes 589832 | tf_op jit(solution)/shard_map/ppermute | solution.py:184
  9.9 1.1 %collective-permute-done = s16[192,512]{1,0:T(8,128)(2,1)S(1)} collective-permute-done((s16[192,512]{1,0:T(8,128)(2,1)S(1)}, s16[192,512]{1,0:T(8,128)(2,1)S(1)}, u32[]{:S(2)}, u32[]{:S(2)}) %collective-permute-start) | collective-permute-done | bytes 196640 | tf_op jit(solution)/shard_map/ppermute | solution.py:184
  11.0 0.1 add.6._
  11.1 3.8 %collective-permute-start.1 = (s16[192,512]{1,0:T(8,128)(2,1)S(1)}, s16[192,512]{1,0:T(8,128)(2,1)S(1)}, u32[]{:S(2)}, u32[]{:S(2)}) collective-permute-start(s16[192,512]{1,0:T(8,128)(2,1)S(1)} %add.6._), channel_id=1, source_target_pairs={{0,64},{64,0},{32,96},{96,32},{1,65},{65,1},{33,97},{97,33},{2,66}... | collective-permute-start | bytes 589832 | tf_op jit(solution)/shard_map/ppermute | solution.py:185
  14.8 0.0 copy-start
  14.8 0.0 copy-start.1
  14.8 5.5 %projection_this_chip.1 = (s16[192,512]{1,0:T(8,128)(2,1)S(1)}, s16[192,512]{1,0:T(8,128)(2,1)S(1)}) custom-call(s32[768,8192]{1,0:T(8,128)} %geno_hbm.3, bf16[8192,512]{1,0:T(8,128)(2,1)S(1)} %get-tuple-element.7.panel_ref, s16[192,512]{1,0:T(8,128)(2,1)S(1)} %add.6._), custom_call_target="tpu_custom_call" | custom-call | flops 3221225472 | bytes 12582912 | tf_op jit(solution)/shard_map/projection_this_chip/pallas_call | solution.py:187
  20.4 0.7 %collective-permute-start.2 = (s16[192,512]{1,0:T(8,128)(2,1)S(1)}, s16[192,512]{1,0:T(8,128)(2,1)S(1)}, u32[]{:S(2)}, u32[]{:S(2)}) collective-permute-start(s16[192,512]{1,0:T(8,128)(2,1)S(1)} %get-tuple-element.11), channel_id=1, source_target_pairs={{0,32},{32,0},{64,96},{96,64},{1,33},{33,1},{65,97},{97,65},{2,34}... | collective-permute-start | bytes 589832 | tf_op jit(solution)/shard_map/ppermute | solution.py:196
  21.1 0.0 collective-permute-done.1
  21.1 0.1 add.7.kept_ref
  21.2 1.0 %collective-permute-done.2.core_ref = s16[192,512]{1,0:T(8,128)(2,1)S(1)} collective-permute-done((s16[192,512]{1,0:T(8,128)(2,1)S(1)}, s16[192,512]{1,0:T(8,128)(2,1)S(1)}, u32[]{:S(2)}, u32[]{:S(2)}) %collective-permute-start.2) | collective-permute-done | bytes 196640 | tf_op jit(solution)/shard_map/ppermute | solution.py:196
  22.2 0.0 copy-done
  22.2 0.3 features.1.own_ref
  22.5 0.5 collective-permute-start.3
  22.9 0.0 copy-done.1
  22.9 0.2 copy.6.pheno_ref
  23.1 0.9 %collective-permute-done.3.other_ref = bf16[192,512]{1,0:T(8,128)(2,1)S(1)} collective-permute-done((bf16[192,512]{1,0:T(8,128)(2,1)S(1)}, bf16[192,512]{1,0:T(8,128)(2,1)S(1)}, u32[]{:S(2)}, u32[]{:S(2)}) %collective-permute-start.3) | collective-permute-done | bytes 196640 | tf_op jit(solution)/shard_map/ppermute | solution.py:205
  24.0 0.5 gram_cross.1
  24.5 16.9 %all_to_all.11 = bf16[32,16,320]{2,1,0:T(8,128)(2,1)S(1)} all-to-all(bf16[32,16,320]{2,1,0:T(8,128)(2,1)S(1)} %bitcast.4), channel_id=1, replica_groups=mesh['marker'=4,'animal'=32] {'animal'}, dimensions={0} | all-to-all | bytes 655360 | tf_op jit(solution)/shard_map/all_to_all | solution.py:214
  41.4 0.1 sum_animals.1.own_ref
  41.5 2.1 %collective-permute-start.4 = (f32[16,320]{1,0:T(8,128)S(1)}, f32[16,320]{1,0:T(8,128)S(1)}, u32[]{:S(2)}, u32[]{:S(2)}) collective-permute-start(f32[16,320]{1,0:T(8,128)S(1)} %sum_animals.1.own_ref), channel_id=1, source_target_pairs={{0,32},{32,0},{64,96},{96,64},{1,33},{33,1},{65,97},{97,65},{2,34}... | collective-permute-start | bytes 61448 | tf_op jit(solution)/shard_map/ppermute | solution.py:223
  43.6 1.8 %collective-permute-start.5 = (f32[16,320]{1,0:T(8,128)S(1)}, f32[16,320]{1,0:T(8,128)S(1)}, u32[]{:S(2)}, u32[]{:S(2)}) collective-permute-start(f32[16,320]{1,0:T(8,128)S(1)} %sum_animals.1.own_ref), channel_id=1, source_target_pairs={{0,64},{64,0},{32,96},{96,32},{1,65},{65,1},{33,97},{97,33},{2,66}... | collective-permute-start | bytes 61448 | tf_op jit(solution)/shard_map/ppermute | solution.py:223
  45.4 1.4 %collective-permute-start.6 = (f32[16,320]{1,0:T(8,128)S(1)}, f32[16,320]{1,0:T(8,128)S(1)}, u32[]{:S(2)}, u32[]{:S(2)}) collective-permute-start(f32[16,320]{1,0:T(8,128)S(1)} %sum_animals.1.own_ref), channel_id=1, source_target_pairs={{0,96},{96,0},{32,64},{64,32},{1,97},{97,1},{33,65},{65,33},{2,98}... | collective-permute-start | bytes 61448 | tf_op jit(solution)/shard_map/ppermute | solution.py:223
  46.8 0.0 collective-permute-done.4.core_ref
  46.8 1.0 %collective-permute-done.5.chip_ref = f32[16,320]{1,0:T(8,128)S(1)} collective-permute-done((f32[16,320]{1,0:T(8,128)S(1)}, f32[16,320]{1,0:T(8,128)S(1)}, u32[]{:S(2)}, u32[]{:S(2)}) %collective-permute-start.5) | collective-permute-done | bytes 20512 | tf_op jit(solution)/shard_map/ppermute | solution.py:223
  47.8 2.3 %collective-permute-done.6.both_ref = f32[16,320]{1,0:T(8,128)S(1)} collective-permute-done((f32[16,320]{1,0:T(8,128)S(1)}, f32[16,320]{1,0:T(8,128)S(1)}, u32[]{:S(2)}, u32[]{:S(2)}) %collective-permute-start.6) | collective-permute-done | bytes 20512 | tf_op jit(solution)/shard_map/ppermute | solution.py:223
  50.1 0.6 %finish.1 = (f32[16,512]{1,0:T(8,128)}, f32[16,64]{1,0:T(8,128)}) custom-call(f32[16,320]{1,0:T(8,128)S(1)} %sum_animals.1.own_ref, f32[16,320]{1,0:T(8,128)S(1)} %collective-permute-done.4.core_ref, f32[16,320]{1,0:T(8,128)S(1)} %collective-permute-done.5.chip_ref, f32[16,320]{1,0:T(8,128)S(1)} %collective-permute-done.6.both_ref), custom_call_target="tpu_custom_call" | custom-call | tf_op jit(solution)/shard_map/finish/pallas_call | solution.py:225
Async XLA Ops:
  8.4 2.6 %collective-permute-start = (s16[192,512]{1,0:T(8,128)(2,1)S(1)}, s16[192,512]{1,0:T(8,128)(2,1)S(1)}, u32[]{:S(2)}, u32[]{:S(2)}) collective-permute-start(s16[192,512]{1,0:T(8,128)(2,1)S(1)} %get-tuple-element.9), channel_id=1, source_target_pairs={{0,32},{32,0},{64,96},{96,64},{1,33},{33,1},{65,97},{97,65},{2,34}... | collective-permute-start | bytes 589832 | tf_op jit(solution)/shard_map/ppermute | solution.py:184
  11.1 10.1 %collective-permute-start.1 = (s16[192,512]{1,0:T(8,128)(2,1)S(1)}, s16[192,512]{1,0:T(8,128)(2,1)S(1)}, u32[]{:S(2)}, u32[]{:S(2)}) collective-permute-start(s16[192,512]{1,0:T(8,128)(2,1)S(1)} %add.6._), channel_id=1, source_target_pairs={{0,64},{64,0},{32,96},{96,32},{1,65},{65,1},{33,97},{97,33},{2,66}... | collective-permute-start | bytes 589832 | tf_op jit(solution)/shard_map/ppermute | solution.py:185
  14.8 7.4 %copy-start = (f32[512]{0:T(512)S(1)}, f32[512]{0:T(512)}, u32[]{:S(2)}) copy-start(f32[512]{0:T(512)} %param.6) | copy-start | bytes 6148
  14.8 8.1 %copy-start.1 = (bf16[768,64]{0,1:T(8,128)(2,1)S(1)}, bf16[768,64]{0,1:T(8,128)(2,1)}, u32[]{:S(2)}) copy-start(bf16[768,64]{0,1:T(8,128)(2,1)} %param.7) | copy-start | bytes 294916
  20.4 1.8 %collective-permute-start.2 = (s16[192,512]{1,0:T(8,128)(2,1)S(1)}, s16[192,512]{1,0:T(8,128)(2,1)S(1)}, u32[]{:S(2)}, u32[]{:S(2)}) collective-permute-start(s16[192,512]{1,0:T(8,128)(2,1)S(1)} %get-tuple-element.11), channel_id=1, source_target_pairs={{0,32},{32,0},{64,96},{96,64},{1,33},{33,1},{65,97},{97,65},{2,34}... | collective-permute-start | bytes 589832 | tf_op jit(solution)/shard_map/ppermute | solution.py:196
  22.5 1.5 %collective-permute-start.3 = (bf16[192,512]{1,0:T(8,128)(2,1)S(1)}, bf16[192,512]{1,0:T(8,128)(2,1)S(1)}, u32[]{:S(2)}, u32[]{:S(2)}) collective-permute-start(bf16[192,512]{1,0:T(8,128)(2,1)S(1)} %features.1.own_ref), channel_id=1, source_target_pairs={{0,32},{32,0},{64,96},{96,64},{1,33},{33,1},{65,97},{97,65},{2,34}... | collective-permute-start | bytes 589832 | tf_op jit(solution)/shard_map/ppermute | solution.py:205
  41.5 5.3 %collective-permute-start.4 = (f32[16,320]{1,0:T(8,128)S(1)}, f32[16,320]{1,0:T(8,128)S(1)}, u32[]{:S(2)}, u32[]{:S(2)}) collective-permute-start(f32[16,320]{1,0:T(8,128)S(1)} %sum_animals.1.own_ref), channel_id=1, source_target_pairs={{0,32},{32,0},{64,96},{96,64},{1,33},{33,1},{65,97},{97,65},{2,34}... | collective-permute-start | bytes 61448 | tf_op jit(solution)/shard_map/ppermute | solution.py:223
  43.6 4.2 %collective-permute-start.5 = (f32[16,320]{1,0:T(8,128)S(1)}, f32[16,320]{1,0:T(8,128)S(1)}, u32[]{:S(2)}, u32[]{:S(2)}) collective-permute-start(f32[16,320]{1,0:T(8,128)S(1)} %sum_animals.1.own_ref), channel_id=1, source_target_pairs={{0,64},{64,0},{32,96},{96,32},{1,65},{65,1},{33,97},{97,33},{2,66}... | collective-permute-start | bytes 61448 | tf_op jit(solution)/shard_map/ppermute | solution.py:223
  45.4 4.8 %collective-permute-start.6 = (f32[16,320]{1,0:T(8,128)S(1)}, f32[16,320]{1,0:T(8,128)S(1)}, u32[]{:S(2)}, u32[]{:S(2)}) collective-permute-start(f32[16,320]{1,0:T(8,128)S(1)} %sum_animals.1.own_ref), channel_id=1, source_target_pairs={{0,96},{96,0},{32,64},{64,32},{1,97},{97,1},{33,65},{65,33},{2,98}... | collective-permute-start | bytes 61448 | tf_op jit(solution)/shard_map/ppermute | solution.py:223

commit v3 on v0

v3 whole, which is shorter than its diff:
```python
import functools
import math

import jax
import jax.numpy as jnp
from jax import lax
from jax.experimental import pallas as pl
from jax.experimental.pallas import tpu as pltpu
from jax.sharding import PartitionSpec as P

OTHER_CORE = [(0, 1), (1, 0), (2, 3), (3, 2)]
OTHER_CHIP = [(0, 2), (2, 0), (1, 3), (3, 1)]
TILE = 256
PARTS = [(0, 512), (512, 512)] + [(1024 * k, 1024) for k in range(1, 7)] + [(7168, 512), (7680, 512)]
AHEAD = (0, 7, 4, 4)
SINE = (-8.88576566829991, 58.46592923637672, -115.4012466635561, 108.25774031408996, -55.913345915340486)


def to_turns(radians):
    steps = jnp.round(radians * (65536.0 / (2.0 * math.pi))).astype(jnp.int32)
    return ((steps << 16) >> 16).astype(jnp.int16)


def copies(geno_hbm, first, geno, sem, parts):
    rows = geno.shape[0]
    return {
        step: pltpu.make_async_copy(
            geno_hbm.at[pl.ds(pl.multiple_of(first, 32), rows), pl.ds(PARTS[step][0], PARTS[step][1])],
            geno.at[:, pl.ds(PARTS[step][0], PARTS[step][1])],
            sem.at[step],
        )
        for step in parts
    }


def row_of(block):
    place = lax.axis_index("marker")
    chip, core = place // 2, place % 2
    other_chip, other_core, quarter_rows, offset, _ = block
    chip = 1 - chip if other_chip else chip
    core = 1 - core if other_core else core
    return (chip * 2 + core) * quarter_rows + offset


def projection_kernel(block, came_parts, next_block, next_parts, loads_panel, *refs):
    refs = list(refs)
    geno_hbm, panel_in = refs.pop(0), refs.pop(0)
    came_ref = refs.pop(0) if came_parts else None
    if not loads_panel:
        refs.pop(0)
    out_ref = refs.pop(0)
    panel_ref = refs.pop(0) if loads_panel else panel_in
    ahead_ref = refs.pop(0) if next_parts else None
    geno, geno_sem, ahead_sem, panel_sem = refs
    came_cols = PARTS[came_parts][0]
    geno_copies = copies(geno_hbm, row_of(block), geno, geno_sem, range(came_parts, len(PARTS)))
    panel_copies = []
    if loads_panel:
        panel_copies = [
            pltpu.make_async_copy(panel_in.at[pl.ds(start, width)], panel_ref.at[pl.ds(start, width)], panel_sem.at[step])
            for step, (start, width) in enumerate(PARTS)
        ]
    ahead_copies = copies(geno_hbm, row_of(next_block), ahead_ref, ahead_sem, range(next_parts)) if next_parts else {}
    for step in range(len(PARTS)):
        if loads_panel:
            panel_copies[step].start()
        if step >= came_parts:
            geno_copies[step].start()
    for copy in ahead_copies.values():
        copy.start()

    def run(*sums):
        for step, (start, width) in enumerate(PARTS):
            if loads_panel:
                panel_copies[step].wait()
            if step >= came_parts:
                geno_copies[step].wait()
            for tile in range(start, start + width, TILE):
                source = came_ref if tile < came_cols else geno
                dosage = (source[:, tile : tile + TILE] - 1).astype(jnp.float32).astype(jnp.bfloat16)
                slot = tile // TILE % 2
                for unit in range(2):
                    pltpu.matmul_push_rhs(panel_ref[tile : tile + TILE, unit * TILE : (unit + 1) * TILE], slot, unit)
                for unit in range(2):
                    pltpu.matmul_acc_lhs(sums[unit], dosage, slot)
        for unit in range(2):
            out_ref[:, unit * TILE : (unit + 1) * TILE] = to_turns(pltpu.matmul_pop(sums[unit]))

    pl.run_scoped(run, *[pltpu.ACC(unit)((geno.shape[0], TILE), jnp.float32) for unit in range(2)])
    for copy in ahead_copies.values():
        copy.wait()


def projection(blocks, ahead, step, geno, panel, came, after=()):
    block, loads_panel = blocks[step], step == 0
    last = step == len(blocks) - 1
    rows, markers, feats = block[-1], geno.shape[1], panel.shape[1]
    next_parts = 0 if last else ahead[step + 1]
    outs = [jax.ShapeDtypeStruct((rows, feats), jnp.int16)]
    if loads_panel:
        outs.append(pltpu.VMEM((markers, feats), jnp.bfloat16))
    if next_parts:
        outs.append(pltpu.VMEM((blocks[step + 1][-1], PARTS[next_parts][0]), jnp.int32))
    operands = [geno, panel] + ([came] if ahead[step] else []) + list(after)
    sems = pltpu.SemaphoreType.DMA((len(PARTS),))
    scratch = rows * markers * 4
    with jax.named_scope(f"projection_block_{step}"):
        made = pl.pallas_call(
            functools.partial(projection_kernel, block, ahead[step], None if last else blocks[step + 1], next_parts, loads_panel),
            out_shape=tuple(outs),
            in_specs=[anywhere(), anywhere() if loads_panel else vmem()] + [vmem()] * bool(ahead[step]) + [anywhere()] * len(after),
            out_specs=(vmem(),) * len(outs),
            scratch_shapes=[pltpu.VMEM((rows, markers), jnp.int32), sems, sems, sems],
            compiler_params=pltpu.CompilerParams(vmem_limit_bytes=scratch + 6 * 2**20),
            cost_estimate=pl.CostEstimate(
                flops=2 * rows * markers * feats, bytes_accessed=scratch + loads_panel * markers * feats * 2, transcendentals=0
            ),
        )(*operands)
    made = list(made)
    return made[0], made[1] if loads_panel else panel, made[-1] if next_parts else None


def features_kernel(kept_ref, core_ref, phase_ref, out_ref):
    turns = kept_ref[...].astype(jnp.int32) + core_ref[...].astype(jnp.int32)
    turns = ((turns << 16) >> 16).astype(jnp.float32) * (1.0 / 65536.0)
    turns = turns + phase_ref[...] * (1.0 / (2.0 * math.pi))
    turns = turns - jnp.round(turns)
    t = jnp.abs(turns) - 0.25
    square = t * t
    value = jnp.full_like(t, SINE[-1])
    for factor in SINE[-2::-1]:
        value = value * square + factor
    out_ref[...] = (value * t).astype(jnp.bfloat16)


def gram_kernel(from_other_core, feature_ref, pheno_ref, *refs):
    out_ref = refs[-1]
    rows, feats = feature_ref.shape
    half = feats // 2
    place = lax.axis_index("marker")
    core = place % 2
    spot = place + 1 - 2 * core if from_other_core else place
    features = feature_ref[...]
    phenotypes = pheno_ref[pl.ds(pl.multiple_of(spot * rows, rows), rows)]

    def product(right):
        return lax.dot_general(features, right, (((0,), (0,)), ((), ())), preferred_element_type=jnp.float32)

    gram = product(feature_ref[:, pl.ds(pl.multiple_of(core * half, half), half)])
    cross = product(phenotypes)
    if not from_other_core:
        out_ref[:, :half] = gram
        out_ref[:, half:] = cross
        return
    gram = gram + refs[0][:, :half]
    cross = cross + refs[0][:, half:]
    high = cross.astype(jnp.bfloat16)
    low = (cross - high.astype(jnp.float32)).astype(jnp.bfloat16)
    out_ref[:, :half] = gram.astype(jnp.bfloat16)
    out_ref[:, half:] = jnp.where(core == 0, high, low)


def sum_kernel(parts, in_ref, out_ref):
    wide = in_ref[...].astype(jnp.float32)
    out_ref[...] = jnp.sum(wide.reshape(parts, wide.shape[0] // parts, wide.shape[1]), axis=0)


def join_kernel(own_ref, other_ref, out_ref):
    core = lax.axis_index("marker") % 2
    out_ref[core] = own_ref[...]
    out_ref[1 - core] = other_ref[...]


def finish_kernel(animals_all, here_ref, there_ref, gram_ref, cross_ref):
    half = gram_ref.shape[1] // 2
    total = here_ref[...] + there_ref[...]
    gram_ref[:, :half] = total[0, :, :half] / animals_all
    gram_ref[:, half:] = total[1, :, :half] / animals_all
    cross_ref[...] = (total[0, :, half:] + total[1, :, half:]) / math.sqrt(animals_all)


def vmem():
    return pl.BlockSpec(memory_space=pltpu.VMEM)


def anywhere():
    return pl.BlockSpec(memory_space=pl.ANY)


def on_device(genotypes, frequencies, phases, phenotypes):
    rows, markers = genotypes.shape
    feats = frequencies.shape[1]
    traits = phenotypes.shape[1]
    groups = lax.axis_size("animal")
    animals_all = float(groups * rows)
    quarter = rows // 4
    small = pltpu.CompilerParams(vmem_limit_bytes=12 * 2**20)
    genotypes = pltpu.with_memory_space_constraint(genotypes, pltpu.HBM)
    frequencies = pltpu.with_memory_space_constraint(frequencies, pltpu.HBM)

    blocks = [(True, True, quarter, 0, quarter), (True, False, quarter, 0, quarter), (False, True, quarter, 0, quarter), (False, False, quarter, 0, quarter)]
    to_core, panel, ahead = projection(blocks, AHEAD, 0, genotypes, frequencies, None)
    received = lax.ppermute(to_core, "marker", OTHER_CORE)
    kept, panel, ahead = projection(blocks, AHEAD, 1, genotypes, panel, ahead, (to_core,))
    to_chip = kept + received
    from_chip = lax.ppermute(to_chip, "marker", OTHER_CHIP)
    to_core, panel, ahead = projection(blocks, AHEAD, 2, genotypes, panel, ahead, (to_chip,))
    from_core = lax.ppermute(to_core, "marker", OTHER_CORE)
    kept, panel, ahead = projection(blocks, AHEAD, 3, genotypes, panel, ahead, (to_core,))
    with jax.named_scope("features"):
        features = pl.pallas_call(
            features_kernel,
            out_shape=jax.ShapeDtypeStruct((quarter, feats), jnp.bfloat16),
            in_specs=[vmem()] * 3,
            out_specs=vmem(),
            compiler_params=small,
        )(kept + from_chip, from_core, phases.reshape(1, feats))
    features_other = lax.ppermute(features, "marker", OTHER_CORE)

    def gram_of(kind, from_other_core, *operands):
        return pl.pallas_call(
            functools.partial(gram_kernel, from_other_core),
            out_shape=jax.ShapeDtypeStruct((feats, feats // 2 + traits), kind),
            in_specs=[vmem()] * len(operands),
            out_specs=vmem(),
            compiler_params=small,
            cost_estimate=pl.CostEstimate(flops=feats * quarter * (feats + 2 * traits), bytes_accessed=0, transcendentals=0),
        )(*operands)

    with jax.named_scope("gram_cross"):
        partial_sums = gram_of(jnp.float32, False, features, phenotypes)
        partial_sums = gram_of(jnp.bfloat16, True, features_other, phenotypes, partial_sums)
    pieces = lax.all_to_all(partial_sums, "animal", 0, 0, tiled=True)
    with jax.named_scope("sum_animals"):
        own = pl.pallas_call(
            functools.partial(sum_kernel, groups),
            out_shape=jax.ShapeDtypeStruct((feats // groups, feats // 2 + traits), jnp.float32),
            in_specs=[vmem()],
            out_specs=vmem(),
            compiler_params=small,
        )(pieces)
    other = lax.ppermute(own, "marker", OTHER_CORE)
    with jax.named_scope("join_cores"):
        here = pl.pallas_call(
            join_kernel,
            out_shape=jax.ShapeDtypeStruct((2,) + own.shape, jnp.float32),
            in_specs=[vmem()] * 2,
            out_specs=vmem(),
            compiler_params=small,
        )(own, other)
    there = lax.ppermute(here, "marker", OTHER_CHIP)
    with jax.named_scope("finish"):
        return pl.pallas_call(
            functools.partial(finish_kernel, animals_all),
            out_shape=(
                jax.ShapeDtypeStruct((feats // groups, feats), jnp.float32),
                jax.ShapeDtypeStruct((feats // groups, traits), jnp.float32),
            ),
            in_specs=[vmem()] * 2,
            out_specs=(vmem(), vmem()),
            compiler_params=small,
        )(here, there)


def solution(mesh):
    in_specs = (P("animal", "marker"), P("marker", None), P(), P("animal", None))
    out_specs = (P("animal", None), P("animal", None))
    return jax.shard_map(
        on_device, mesh=mesh, in_specs=in_specs, out_specs=out_specs, check_vma=False
    )
```

time: 255 us -> 49.3 us (0.19)
  the two profiles are of different devices: /device:TPU:0 before, /device:TPU:1 now
where the time goes in v3:
time: 49.3 us; the launch traced here: 49.1 us
  Pallas kernels  17.1 us (35%)
  blocking collectives  17.1 us (35%)
  starting transfers between devices  10.3 us (21%)
  waiting for transfers between devices  3.53 us (7%)
  between operations  0.73 us (1%)
    all_to_all x1, blocking collectives, on_device(): pieces = lax.all_to_all(partial_sums, 'animal', 0, 0, tiled=True)  17.1 us
    pallas_call x4, Pallas kernels, projection(): pl.pallas_call(functools.partial(projection_kernel, block, ahead[step], N...  15.5 us
    ppermute x1, starting transfers between devices, on_device(): from_chip = lax.ppermute(to_chip, 'marker', OTHER_CHIP)  3.76 us
    ppermute x1, starting transfers between devices, on_device(): there = lax.ppermute(here, 'marker', OTHER_CHIP)  2.5 us
    ppermute x1, waiting for transfers between devices, on_device(): there = lax.ppermute(here, 'marker', OTHER_CHIP)  1.95 us
    ppermute x1, starting transfers between devices, on_device(): other = lax.ppermute(own, 'marker', OTHER_CORE)  1.92 us
    ppermute x1, starting transfers between devices, on_device(): received = lax.ppermute(to_core, 'marker', OTHER_CORE)  1.5 us
  transfers between devices with their start and end apart: 6, of which 3 were waited for; matrix products, arithmetic and copies ran while one was open for 0% of the time, Pallas kernels for 18%

profile of v3, /device:TPU:1, one launch (start us, length us, event | category | flops | bytes accessed | tf_op | source)
XLA Modules:
  0.0 49.1 jit_solution(11289181219129723730)
XLA Ops:
  0.6 6.9 %projection_block_0.1 = (s16[192,512]{1,0:T(8,128)(2,1)S(1)}, bf16[8192,512]{1,0:T(8,128)(2,1)S(1)}, s32[192,6144]{1,0:T(8,128)S(1)}) custom-call(s32[768,8192]{1,0:T(8,128)} %refs_0_.7, bf16[8192,512]{1,0:T(8,128)(2,1)} %refs_1_.1), custom_call_target="tpu_custom_call" | custom-call | flops 1610612736 | bytes 14680064 | tf_op jit(solution)/shard_map/projection_block_0/pallas_call | solution.py:108
  7.5 1.5 %collective-permute-start = (s16[192,512]{1,0:T(8,128)(2,1)S(1)}, s16[192,512]{1,0:T(8,128)(2,1)S(1)}, u32[]{:S(2)}, u32[]{:S(2)}) collective-permute-start(s16[192,512]{1,0:T(8,128)(2,1)S(1)} %get-tuple-element.11.refs_3_), channel_id=1, source_target_pairs={{0,32},{32,0},{64,96},{96,64},{1,33},{33,1},{65,97},{97,65},{2,34}... | collective-permute-start | bytes 589832 | tf_op jit(solution)/shard_map/ppermute | solution.py:203
  9.0 2.4 %projection_block_1.1 = (s16[192,512]{1,0:T(8,128)(2,1)S(1)}, s32[192,3072]{1,0:T(8,128)S(1)}) custom-call(s32[768,8192]{1,0:T(8,128)} %refs_0_.7, bf16[8192,512]{1,0:T(8,128)(2,1)S(1)} %get-tuple-element.9.refs_1_, s32[192,6144]{1,0:T(8,128)S(1)} %get-tuple-element.10.refs_2_, s16[192,512]{1,0:T(8,128)(2,1)S(1)} %get-tuple-element.11.refs_3_), custom_call_target="tpu_custom_call" | custom-call | flops 1610612736 | bytes 6291456 | tf_op jit(solution)/shard_map/projection_block_1/pallas_call | solution.py:108
  11.4 0.0 collective-permute-done
  11.4 0.1 add.6.refs_3_
  11.5 3.8 %collective-permute-start.1 = (s16[192,512]{1,0:T(8,128)(2,1)S(1)}, s16[192,512]{1,0:T(8,128)(2,1)S(1)}, u32[]{:S(2)}, u32[]{:S(2)}) collective-permute-start(s16[192,512]{1,0:T(8,128)(2,1)S(1)} %add.6.refs_3_), channel_id=1, source_target_pairs={{0,64},{64,0},{32,96},{96,32},{1,65},{65,1},{33,97},{97,33},{2,66}... | collective-permute-start | bytes 589832 | tf_op jit(solution)/shard_map/ppermute | solution.py:206
  15.3 3.1 %projection_block_2.1 = (s16[192,512]{1,0:T(8,128)(2,1)S(1)}, s32[192,3072]{1,0:T(8,128)S(1)}) custom-call(s32[768,8192]{1,0:T(8,128)} %refs_0_.7, bf16[8192,512]{1,0:T(8,128)(2,1)S(1)} %get-tuple-element.9.refs_1_, s32[192,3072]{1,0:T(8,128)S(1)} %get-tuple-element.12.refs_2_, s16[192,512]{1,0:T(8,128)(2,1)S(1)} %add.6.refs_3_), custom_call_target="tpu_custom_call" | custom-call | flops 1610612736 | bytes 6291456 | tf_op jit(solution)/shard_map/projection_block_2/pallas_call | solution.py:108
  18.4 0.4 collective-permute-start.2
  18.8 0.0 copy-start
  18.8 0.0 copy-start.1
  18.8 3.0 %projection_block_3.1 = s16[192,512]{1,0:T(8,128)(2,1)S(1)} custom-call(s32[768,8192]{1,0:T(8,128)} %refs_0_.7, bf16[8192,512]{1,0:T(8,128)(2,1)S(1)} %get-tuple-element.9.refs_1_, s32[192,3072]{1,0:T(8,128)S(1)} %get-tuple-element.14.refs_2_, s16[192,512]{1,0:T(8,128)(2,1)S(1)} %get-tuple-element.15.refs_3_), custom_call_target="tpu_custom_call" | custom-call | flops 1610612736 | bytes 6291456 | tf_op jit(solution)/shard_map/projection_block_3/pallas_call | solution.py:108
  21.8 0.0 collective-permute-done.1
  21.8 0.1 add.7.kept_ref
  21.9 0.0 collective-permute-done.2.core_ref
  21.9 0.0 copy-done
  21.9 0.3 features.1.feature_ref
  22.2 0.3 collective-permute-start.3
  22.5 0.0 copy-done.1
  22.5 0.2 copy.7.pheno_ref
  22.7 0.3 gram_cross.2.refs_0_
  23.0 0.7 %collective-permute-done.3.feature_ref = bf16[192,512]{1,0:T(8,128)(2,1)S(1)} collective-permute-done((bf16[192,512]{1,0:T(8,128)(2,1)S(1)}, bf16[192,512]{1,0:T(8,128)(2,1)S(1)}, u32[]{:S(2)}, u32[]{:S(2)}) %collective-permute-start.3) | collective-permute-done | bytes 196640 | tf_op jit(solution)/shard_map/ppermute | solution.py:218
  23.7 0.3 gram_cross.3
  24.1 17.1 %all_to_all.11 = bf16[32,16,320]{2,1,0:T(8,128)(2,1)S(1)} all-to-all(bf16[32,16,320]{2,1,0:T(8,128)(2,1)S(1)} %bitcast.4), channel_id=1, replica_groups=mesh['marker'=4,'animal'=32] {'animal'}, dimensions={0} | all-to-all | bytes 655360 | tf_op jit(solution)/shard_map/all_to_all | solution.py:233
  41.2 0.1 sum_animals.1.own_ref
  41.2 1.9 %collective-permute-start.4 = (f32[16,320]{1,0:T(8,128)S(1)}, f32[16,320]{1,0:T(8,128)S(1)}, u32[]{:S(2)}, u32[]{:S(2)}) collective-permute-start(f32[16,320]{1,0:T(8,128)S(1)} %sum_animals.1.own_ref), channel_id=1, source_target_pairs={{0,32},{32,0},{64,96},{96,64},{1,33},{33,1},{65,97},{97,65},{2,34}... | collective-permute-start | bytes 61448 | tf_op jit(solution)/shard_map/ppermute | solution.py:242
  43.2 0.8 %collective-permute-done.4.other_ref = f32[16,320]{1,0:T(8,128)S(1)} collective-permute-done((f32[16,320]{1,0:T(8,128)S(1)}, f32[16,320]{1,0:T(8,128)S(1)}, u32[]{:S(2)}, u32[]{:S(2)}) %collective-permute-start.4) | collective-permute-done | bytes 20512 | tf_op jit(solution)/shard_map/ppermute | solution.py:242
  44.0 2.5 %collective-permute-start.5 = (f32[2,16,320]{2,1,0:T(8,128)S(1)}, f32[2,16,320]{2,1,0:T(8,128)S(1)}, u32[]{:S(2)}, u32[]{:S(2)}) collective-permute-start(f32[2,16,320]{2,1,0:T(8,128)S(1)} %join_cores.1.here_ref), channel_id=1, source_target_pairs={{0,64},{64,0},{32,96},{96,32},{1,65},{65,1},{33,97},{97,33},{2,66}... | collective-permute-start | bytes 122888 | tf_op jit(solution)/shard_map/ppermute | solution.py:251
  46.5 1.9 %collective-permute-done.5.there_ref = f32[2,16,320]{2,1,0:T(8,128)S(1)} collective-permute-done((f32[2,16,320]{2,1,0:T(8,128)S(1)}, f32[2,16,320]{2,1,0:T(8,128)S(1)}, u32[]{:S(2)}, u32[]{:S(2)}) %collective-permute-start.5) | collective-permute-done | bytes 40992 | tf_op jit(solution)/shard_map/ppermute | solution.py:251
  48.5 0.6 %finish.1 = (f32[16,512]{1,0:T(8,128)}, f32[16,64]{1,0:T(8,128)}) custom-call(f32[2,16,320]{2,1,0:T(8,128)S(1)} %join_cores.1.here_ref, f32[2,16,320]{2,1,0:T(8,128)S(1)} %collective-permute-done.5.there_ref), custom_call_target="tpu_custom_call" | custom-call | tf_op jit(solution)/shard_map/finish/pallas_call | solution.py:253
  (1 shorter events, 0.0 us)
Async XLA Ops:
  7.5 3.9 %collective-permute-start = (s16[192,512]{1,0:T(8,128)(2,1)S(1)}, s16[192,512]{1,0:T(8,128)(2,1)S(1)}, u32[]{:S(2)}, u32[]{:S(2)}) collective-permute-start(s16[192,512]{1,0:T(8,128)(2,1)S(1)} %get-tuple-element.11.refs_3_), channel_id=1, source_target_pairs={{0,32},{32,0},{64,96},{96,64},{1,33},{33,1},{65,97},{97,65},{2,34}... | collective-permute-start | bytes 589832 | tf_op jit(solution)/shard_map/ppermute | solution.py:203
  11.5 10.3 %collective-permute-start.1 = (s16[192,512]{1,0:T(8,128)(2,1)S(1)}, s16[192,512]{1,0:T(8,128)(2,1)S(1)}, u32[]{:S(2)}, u32[]{:S(2)}) collective-permute-start(s16[192,512]{1,0:T(8,128)(2,1)S(1)} %add.6.refs_3_), channel_id=1, source_target_pairs={{0,64},{64,0},{32,96},{96,32},{1,65},{65,1},{33,97},{97,33},{2,66}... | collective-permute-start | bytes 589832 | tf_op jit(solution)/shard_map/ppermute | solution.py:206
  18.4 3.5 %collective-permute-start.2 = (s16[192,512]{1,0:T(8,128)(2,1)S(1)}, s16[192,512]{1,0:T(8,128)(2,1)S(1)}, u32[]{:S(2)}, u32[]{:S(2)}) collective-permute-start(s16[192,512]{1,0:T(8,128)(2,1)S(1)} %get-tuple-element.15.refs_3_), channel_id=1, source_target_pairs={{0,32},{32,0},{64,96},{96,64},{1,33},{33,1},{65,97},{97,65},{2,34}... | collective-permute-start | bytes 589832 | tf_op jit(solution)/shard_map/ppermute | solution.py:208
  18.8 3.1 %copy-start = (f32[512]{0:T(512)S(1)}, f32[512]{0:T(512)}, u32[]{:S(2)}) copy-start(f32[512]{0:T(512)} %param.6) | copy-start | bytes 6148
  18.8 3.7 %copy-start.1 = (bf16[768,64]{0,1:T(8,128)(2,1)S(1)}, bf16[768,64]{0,1:T(8,128)(2,1)}, u32[]{:S(2)}) copy-start(bf16[768,64]{0,1:T(8,128)(2,1)} %param.7) | copy-start | bytes 294916
  22.2 1.5 %collective-permute-start.3 = (bf16[192,512]{1,0:T(8,128)(2,1)S(1)}, bf16[192,512]{1,0:T(8,128)(2,1)S(1)}, u32[]{:S(2)}, u32[]{:S(2)}) collective-permute-start(bf16[192,512]{1,0:T(8,128)(2,1)S(1)} %features.1.feature_ref), channel_id=1, source_target_pairs={{0,32},{32,0},{64,96},{96,64},{1,33},{33,1},{65,97},{97,65},{2,34}... | collective-permute-start | bytes 589832 | tf_op jit(solution)/shard_map/ppermute | solution.py:218
  41.2 2.8 %collective-permute-start.4 = (f32[16,320]{1,0:T(8,128)S(1)}, f32[16,320]{1,0:T(8,128)S(1)}, u32[]{:S(2)}, u32[]{:S(2)}) collective-permute-start(f32[16,320]{1,0:T(8,128)S(1)} %sum_animals.1.own_ref), channel_id=1, source_target_pairs={{0,32},{32,0},{64,96},{96,64},{1,33},{33,1},{65,97},{97,65},{2,34}... | collective-permute-start | bytes 61448 | tf_op jit(solution)/shard_map/ppermute | solution.py:242
  44.0 4.4 %collective-permute-start.5 = (f32[2,16,320]{2,1,0:T(8,128)S(1)}, f32[2,16,320]{2,1,0:T(8,128)S(1)}, u32[]{:S(2)}, u32[]{:S(2)}) collective-permute-start(f32[2,16,320]{2,1,0:T(8,128)S(1)} %join_cores.1.here_ref), channel_id=1, source_target_pairs={{0,64},{64,0},{32,96},{96,32},{1,65},{65,1},{33,97},{97,33},{2,66}... | collective-permute-start | bytes 122888 | tf_op jit(solution)/shard_map/ppermute | solution.py:251

commit v4 on v3

--- a/solution.py
+++ b/solution.py
@@ -11,8 +11,8 @@
 OTHER_CORE = [(0, 1), (1, 0), (2, 3), (3, 2)]
 OTHER_CHIP = [(0, 2), (2, 0), (1, 3), (3, 1)]
 TILE = 256
-PARTS = [(0, 512), (512, 512)] + [(1024 * k, 1024) for k in range(1, 7)] + [(7168, 512), (7680, 512)]
-AHEAD = (0, 7, 4, 4)
+PARTS = [(0, 1024), (1024, 1024), (2048, 2048), (4096, 2048), (6144, 1536), (7680, 512)]
+AHEAD = (0, 4, 2, 3)
 SINE = (-8.88576566829991, 58.46592923637672, -115.4012466635561, 108.25774031408996, -55.913345915340486)
 
 

time: 49.3 us -> 49 us (level)
  no operation moved by 1% of the time
where the time goes in v4:
time: 49 us; the launch traced here: 48.8 us
  blocking collectives  17 us (35%)
  Pallas kernels  16.8 us (34%)
  starting transfers between devices  10.3 us (21%)
  waiting for transfers between devices  3.63 us (7%)
  between operations  0.73 us (1%)
    all_to_all x1, blocking collectives, on_device(): pieces = lax.all_to_all(partial_sums, 'animal', 0, 0, tiled=True)  17 us
    pallas_call x4, Pallas kernels, projection(): pl.pallas_call(functools.partial(projection_kernel, block, ahead[step], N...  15.1 us
    ppermute x1, starting transfers between devices, on_device(): from_chip = lax.ppermute(to_chip, 'marker', OTHER_CHIP)  3.76 us
    ppermute x1, starting transfers between devices, on_device(): there = lax.ppermute(here, 'marker', OTHER_CHIP)  2.39 us
    ppermute x1, waiting for transfers between devices, on_device(): there = lax.ppermute(here, 'marker', OTHER_CHIP)  2.05 us
    ppermute x1, starting transfers between devices, on_device(): other = lax.ppermute(own, 'marker', OTHER_CORE)  2 us
    ppermute x1, starting transfers between devices, on_device(): received = lax.ppermute(to_core, 'marker', OTHER_CORE)  1.5 us
  transfers between devices with their start and end apart: 6, of which 3 were waited for; matrix products, arithmetic and copies ran while one was open for 0% of the time, Pallas kernels for 18%

profile of v4, /device:TPU:1, one launch (start us, length us, event | category | flops | bytes accessed | tf_op | source)
XLA Modules:
  0.0 48.8 jit_solution(9855142958537371495)
XLA Ops:
  0.6 6.8 %projection_block_0.1 = (s16[192,512]{1,0:T(8,128)(2,1)S(1)}, bf16[8192,512]{1,0:T(8,128)(2,1)S(1)}, s32[192,6144]{1,0:T(8,128)S(1)}) custom-call(s32[768,8192]{1,0:T(8,128)} %refs_0_.7, bf16[8192,512]{1,0:T(8,128)(2,1)} %refs_1_.1), custom_call_target="tpu_custom_call" | custom-call | flops 1610612736 | bytes 14680064 | tf_op jit(solution)/shard_map/projection_block_0/pallas_call | solution.py:108
  7.4 1.5 %collective-permute-start = (s16[192,512]{1,0:T(8,128)(2,1)S(1)}, s16[192,512]{1,0:T(8,128)(2,1)S(1)}, u32[]{:S(2)}, u32[]{:S(2)}) collective-permute-start(s16[192,512]{1,0:T(8,128)(2,1)S(1)} %get-tuple-element.11.refs_3_), channel_id=1, source_target_pairs={{0,32},{32,0},{64,96},{96,64},{1,33},{33,1},{65,97},{97,65},{2,34}... | collective-permute-start | bytes 589832 | tf_op jit(solution)/shard_map/ppermute | solution.py:203
  8.9 2.1 %projection_block_1.1 = (s16[192,512]{1,0:T(8,128)(2,1)S(1)}, s32[192,2048]{1,0:T(8,128)S(1)}) custom-call(s32[768,8192]{1,0:T(8,128)} %refs_0_.7, bf16[8192,512]{1,0:T(8,128)(2,1)S(1)} %get-tuple-element.9.refs_1_, s32[192,6144]{1,0:T(8,128)S(1)} %get-tuple-element.10.refs_2_, s16[192,512]{1,0:T(8,128)(2,1)S(1)} %get-tuple-element.11.refs_3_), custom_call_target="tpu_custom_call" | custom-call | flops 1610612736 | bytes 6291456 | tf_op jit(solution)/shard_map/projection_block_1/pallas_call | solution.py:108
  11.0 0.0 collective-permute-done
  11.0 0.1 add.6.refs_3_
  11.1 3.8 %collective-permute-start.1 = (s16[192,512]{1,0:T(8,128)(2,1)S(1)}, s16[192,512]{1,0:T(8,128)(2,1)S(1)}, u32[]{:S(2)}, u32[]{:S(2)}) collective-permute-start(s16[192,512]{1,0:T(8,128)(2,1)S(1)} %add.6.refs_3_), channel_id=1, source_target_pairs={{0,64},{64,0},{32,96},{96,32},{1,65},{65,1},{33,97},{97,33},{2,66}... | collective-permute-start | bytes 589832 | tf_op jit(solution)/shard_map/ppermute | solution.py:206
  14.9 3.5 %projection_block_2.1 = (s16[192,512]{1,0:T(8,128)(2,1)S(1)}, s32[192,4096]{1,0:T(8,128)S(1)}) custom-call(s32[768,8192]{1,0:T(8,128)} %refs_0_.7, bf16[8192,512]{1,0:T(8,128)(2,1)S(1)} %get-tuple-element.9.refs_1_, s32[192,2048]{1,0:T(8,128)S(1)} %get-tuple-element.12.refs_2_, s16[192,512]{1,0:T(8,128)(2,1)S(1)} %add.6.refs_3_), custom_call_target="tpu_custom_call" | custom-call | flops 1610612736 | bytes 6291456 | tf_op jit(solution)/shard_map/projection_block_2/pallas_call | solution.py:108
  18.4 0.4 collective-permute-start.2
  18.7 0.0 copy-start
  18.7 0.0 copy-start.1
  18.7 2.8 %projection_block_3.1 = s16[192,512]{1,0:T(8,128)(2,1)S(1)} custom-call(s32[768,8192]{1,0:T(8,128)} %refs_0_.7, bf16[8192,512]{1,0:T(8,128)(2,1)S(1)} %get-tuple-element.9.refs_1_, s32[192,4096]{1,0:T(8,128)S(1)} %get-tuple-element.14.refs_2_, s16[192,512]{1,0:T(8,128)(2,1)S(1)} %get-tuple-element.15.refs_3_), custom_call_target="tpu_custom_call" | custom-call | flops 1610612736 | bytes 6291456 | tf_op jit(solution)/shard_map/projection_block_3/pallas_call | solution.py:108
  21.5 0.0 collective-permute-done.1
  21.5 0.1 add.7.kept_ref
  21.6 0.0 collective-permute-done.2.core_ref
  21.6 0.0 copy-done
  21.6 0.3 features.1.feature_ref
  21.9 0.3 collective-permute-start.3
  22.2 0.0 copy-done.1
  22.2 0.2 copy.7.pheno_ref
  22.4 0.3 gram_cross.2.refs_0_
  22.7 0.7 %collective-permute-done.3.feature_ref = bf16[192,512]{1,0:T(8,128)(2,1)S(1)} collective-permute-done((bf16[192,512]{1,0:T(8,128)(2,1)S(1)}, bf16[192,512]{1,0:T(8,128)(2,1)S(1)}, u32[]{:S(2)}, u32[]{:S(2)}) %collective-permute-start.3) | collective-permute-done | bytes 196640 | tf_op jit(solution)/shard_map/ppermute | solution.py:218
  23.4 0.3 gram_cross.3
  23.8 17.0 %all_to_all.11 = bf16[32,16,320]{2,1,0:T(8,128)(2,1)S(1)} all-to-all(bf16[32,16,320]{2,1,0:T(8,128)(2,1)S(1)} %bitcast.4), channel_id=1, replica_groups=mesh['marker'=4,'animal'=32] {'animal'}, dimensions={0} | all-to-all | bytes 655360 | tf_op jit(solution)/shard_map/all_to_all | solution.py:233
  40.8 0.1 sum_animals.1.own_ref
  40.8 2.0 %collective-permute-start.4 = (f32[16,320]{1,0:T(8,128)S(1)}, f32[16,320]{1,0:T(8,128)S(1)}, u32[]{:S(2)}, u32[]{:S(2)}) collective-permute-start(f32[16,320]{1,0:T(8,128)S(1)} %sum_animals.1.own_ref), channel_id=1, source_target_pairs={{0,32},{32,0},{64,96},{96,64},{1,33},{33,1},{65,97},{97,65},{2,34}... | collective-permute-start | bytes 61448 | tf_op jit(solution)/shard_map/ppermute | solution.py:242
  42.8 0.8 %collective-permute-done.4.other_ref = f32[16,320]{1,0:T(8,128)S(1)} collective-permute-done((f32[16,320]{1,0:T(8,128)S(1)}, f32[16,320]{1,0:T(8,128)S(1)}, u32[]{:S(2)}, u32[]{:S(2)}) %collective-permute-start.4) | collective-permute-done | bytes 20512 | tf_op jit(solution)/shard_map/ppermute | solution.py:242
  43.7 2.4 %collective-permute-start.5 = (f32[2,16,320]{2,1,0:T(8,128)S(1)}, f32[2,16,320]{2,1,0:T(8,128)S(1)}, u32[]{:S(2)}, u32[]{:S(2)}) collective-permute-start(f32[2,16,320]{2,1,0:T(8,128)S(1)} %join_cores.1.here_ref), channel_id=1, source_target_pairs={{0,64},{64,0},{32,96},{96,32},{1,65},{65,1},{33,97},{97,33},{2,66}... | collective-permute-start | bytes 122888 | tf_op jit(solution)/shard_map/ppermute | solution.py:251
  46.1 2.0 %collective-permute-done.5.there_ref = f32[2,16,320]{2,1,0:T(8,128)S(1)} collective-permute-done((f32[2,16,320]{2,1,0:T(8,128)S(1)}, f32[2,16,320]{2,1,0:T(8,128)S(1)}, u32[]{:S(2)}, u32[]{:S(2)}) %collective-permute-start.5) | collective-permute-done | bytes 40992 | tf_op jit(solution)/shard_map/ppermute | solution.py:251
  48.1 0.6 %finish.1 = (f32[16,512]{1,0:T(8,128)}, f32[16,64]{1,0:T(8,128)}) custom-call(f32[2,16,320]{2,1,0:T(8,128)S(1)} %join_cores.1.here_ref, f32[2,16,320]{2,1,0:T(8,128)S(1)} %collective-permute-done.5.there_ref), custom_call_target="tpu_custom_call" | custom-call | tf_op jit(solution)/shard_map/finish/pallas_call | solution.py:253
  (1 shorter events, 0.0 us)
Async XLA Ops:
  7.4 3.6 %collective-permute-start = (s16[192,512]{1,0:T(8,128)(2,1)S(1)}, s16[192,512]{1,0:T(8,128)(2,1)S(1)}, u32[]{:S(2)}, u32[]{:S(2)}) collective-permute-start(s16[192,512]{1,0:T(8,128)(2,1)S(1)} %get-tuple-element.11.refs_3_), channel_id=1, source_target_pairs={{0,32},{32,0},{64,96},{96,64},{1,33},{33,1},{65,97},{97,65},{2,34}... | collective-permute-start | bytes 589832 | tf_op jit(solution)/shard_map/ppermute | solution.py:203
  11.1 10.4 %collective-permute-start.1 = (s16[192,512]{1,0:T(8,128)(2,1)S(1)}, s16[192,512]{1,0:T(8,128)(2,1)S(1)}, u32[]{:S(2)}, u32[]{:S(2)}) collective-permute-start(s16[192,512]{1,0:T(8,128)(2,1)S(1)} %add.6.refs_3_), channel_id=1, source_target_pairs={{0,64},{64,0},{32,96},{96,32},{1,65},{65,1},{33,97},{97,33},{2,66}... | collective-permute-start | bytes 589832 | tf_op jit(solution)/shard_map/ppermute | solution.py:206
  18.4 3.2 %collective-permute-start.2 = (s16[192,512]{1,0:T(8,128)(2,1)S(1)}, s16[192,512]{1,0:T(8,128)(2,1)S(1)}, u32[]{:S(2)}, u32[]{:S(2)}) collective-permute-start(s16[192,512]{1,0:T(8,128)(2,1)S(1)} %get-tuple-element.15.refs_3_), channel_id=1, source_target_pairs={{0,32},{32,0},{64,96},{96,64},{1,33},{33,1},{65,97},{97,65},{2,34}... | collective-permute-start | bytes 589832 | tf_op jit(solution)/shard_map/ppermute | solution.py:208
  18.7 2.9 %copy-start = (f32[512]{0:T(512)S(1)}, f32[512]{0:T(512)}, u32[]{:S(2)}) copy-start(f32[512]{0:T(512)} %param.6) | copy-start | bytes 6148
  18.7 3.5 %copy-start.1 = (bf16[768,64]{0,1:T(8,128)(2,1)S(1)}, bf16[768,64]{0,1:T(8,128)(2,1)}, u32[]{:S(2)}) copy-start(bf16[768,64]{0,1:T(8,128)(2,1)} %param.7) | copy-start | bytes 294916
  21.9 1.5 %collective-permute-start.3 = (bf16[192,512]{1,0:T(8,128)(2,1)S(1)}, bf16[192,512]{1,0:T(8,128)(2,1)S(1)}, u32[]{:S(2)}, u32[]{:S(2)}) collective-permute-start(bf16[192,512]{1,0:T(8,128)(2,1)S(1)} %features.1.feature_ref), channel_id=1, source_target_pairs={{0,32},{32,0},{64,96},{96,64},{1,33},{33,1},{65,97},{97,65},{2,34}... | collective-permute-start | bytes 589832 | tf_op jit(solution)/shard_map/ppermute | solution.py:218
  40.8 2.9 %collective-permute-start.4 = (f32[16,320]{1,0:T(8,128)S(1)}, f32[16,320]{1,0:T(8,128)S(1)}, u32[]{:S(2)}, u32[]{:S(2)}) collective-permute-start(f32[16,320]{1,0:T(8,128)S(1)} %sum_animals.1.own_ref), channel_id=1, source_target_pairs={{0,32},{32,0},{64,96},{96,64},{1,33},{33,1},{65,97},{97,65},{2,34}... | collective-permute-start | bytes 61448 | tf_op jit(solution)/shard_map/ppermute | solution.py:242
  43.7 4.4 %collective-permute-start.5 = (f32[2,16,320]{2,1,0:T(8,128)S(1)}, f32[2,16,320]{2,1,0:T(8,128)S(1)}, u32[]{:S(2)}, u32[]{:S(2)}) collective-permute-start(f32[2,16,320]{2,1,0:T(8,128)S(1)} %join_cores.1.here_ref), channel_id=1, source_target_pairs={{0,64},{64,0},{32,96},{96,32},{1,65},{65,1},{33,97},{97,33},{2,66}... | collective-permute-start | bytes 122888 | tf_op jit(solution)/shard_map/ppermute | solution.py:251

commit v5 on v4

--- a/solution.py
+++ b/solution.py
@@ -11,6 +11,7 @@
 OTHER_CORE = [(0, 1), (1, 0), (2, 3), (3, 2)]
 OTHER_CHIP = [(0, 2), (2, 0), (1, 3), (3, 1)]
 TILE = 256
+LANES = 128
 PARTS = [(0, 1024), (1024, 1024), (2048, 2048), (4096, 2048), (6144, 1536), (7680, 512)]
 AHEAD = (0, 4, 2, 3)
 SINE = (-8.88576566829991, 58.46592923637672, -115.4012466635561, 108.25774031408996, -55.913345915340486)
@@ -152,17 +153,21 @@
         out_ref[:, :half] = gram
         out_ref[:, half:] = cross
         return
-    gram = gram + refs[0][:, :half]
-    cross = cross + refs[0][:, half:]
+    pieces = out_ref.shape[0]
+    height = feats // pieces
+    gram = (gram + refs[0][:, :half]).astype(jnp.bfloat16)
+    cross = (cross + refs[0][:, half:]).reshape(pieces, 2, height // 2, LANES)
+    left = lax.broadcasted_iota(jnp.int32, (pieces, height // 2, LANES), 2) < LANES // 2
+    cross = jnp.where(left, cross[:, 0], cross[:, 1])
     high = cross.astype(jnp.bfloat16)
     low = (cross - high.astype(jnp.float32)).astype(jnp.bfloat16)
-    out_ref[:, :half] = gram.astype(jnp.bfloat16)
-    out_ref[:, half:] = jnp.where(core == 0, high, low)
-
-
-def sum_kernel(parts, in_ref, out_ref):
-    wide = in_ref[...].astype(jnp.float32)
-    out_ref[...] = jnp.sum(wide.reshape(parts, wide.shape[0] // parts, wide.shape[1]), axis=0)
+    out_ref[:, :height] = gram[:, :LANES].reshape(pieces, height, LANES)
+    out_ref[:, height : 2 * height] = gram[:, LANES:].reshape(pieces, height, LANES)
+    out_ref[:, 2 * height :] = jnp.where(core == 0, high, low)
+
+
+def sum_kernel(in_ref, out_ref):
+    out_ref[...] = jnp.sum(in_ref[...].astype(jnp.float32), axis=0)
 
 
 def join_kernel(own_ref, other_ref, out_ref):
@@ -172,11 +177,15 @@
 
 
 def finish_kernel(animals_all, here_ref, there_ref, gram_ref, cross_ref):
-    half = gram_ref.shape[1] // 2
+    height = gram_ref.shape[0]
     total = here_ref[...] + there_ref[...]
-    gram_ref[:, :half] = total[0, :, :half] / animals_all
-    gram_ref[:, half:] = total[1, :, :half] / animals_all
-    cross_ref[...] = (total[0, :, half:] + total[1, :, half:]) / math.sqrt(animals_all)
+    for core in range(2):
+        for part in range(2):
+            start = (2 * core + part) * LANES
+            gram_ref[:, start : start + LANES] = total[core, part * height : (part + 1) * height] / animals_all
+    cross = (total[0, 2 * height :] + total[1, 2 * height :]) / math.sqrt(animals_all)
+    cross_ref[: height // 2] = cross[:, : LANES // 2]
+    cross_ref[height // 2 :] = cross[:, LANES // 2 :]
 
 
 def vmem():
@@ -217,24 +226,30 @@
         )(kept + from_chip, from_core, phases.reshape(1, feats))
     features_other = lax.ppermute(features, "marker", OTHER_CORE)
 
-    def gram_of(kind, from_other_core, *operands):
+    height = feats // groups
+    piece = (2 * height + height // 2, LANES)
+
+    def gram_of(from_other_core, out_shape, *operands):
         return pl.pallas_call(
             functools.partial(gram_kernel, from_other_core),
-            out_shape=jax.ShapeDtypeStruct((feats, feats // 2 + traits), kind),
+            out_shape=out_shape,
             in_specs=[vmem()] * len(operands),
             out_specs=vmem(),
             compiler_params=small,
-            cost_estimate=pl.CostEstimate(flops=feats * quarter * (feats + 2 * traits), bytes_accessed=0, transcendentals=0),
+            cost_estimate=pl.CostEstimate(flops=feats * quarter * (feats + 2 * LANES), bytes_accessed=0, transcendentals=0),
         )(*operands)
 
     with jax.named_scope("gram_cross"):
-        partial_sums = gram_of(jnp.float32, False, features, phenotypes)
-        partial_sums = gram_of(jnp.bfloat16, True, features_other, phenotypes, partial_sums)
-    pieces = lax.all_to_all(partial_sums, "animal", 0, 0, tiled=True)
+        twice = jnp.concatenate([phenotypes, phenotypes], axis=1)
+        partial_sums = gram_of(False, jax.ShapeDtypeStruct((feats, feats // 2 + LANES), jnp.float32), features, twice)
+        partial_sums = gram_of(
+            True, jax.ShapeDtypeStruct((groups,) + piece, jnp.bfloat16), features_other, twice, partial_sums
+        )
+    pieces = lax.all_to_all(partial_sums, "animal", 0, 0)
     with jax.named_scope("sum_animals"):
         own = pl.pallas_call(
-            functools.partial(sum_kernel, groups),
-            out_shape=jax.ShapeDtypeStruct((feats // groups, feats // 2 + traits), jnp.float32),
+            sum_kernel,
+            out_shape=jax.ShapeDtypeStruct(piece, jnp.float32),
             in_specs=[vmem()],
             out_specs=vmem(),
             compiler_params=small,

time: 49 us -> 48 us (0.980)
  blocking collectives: 17 us -> 16.5 us
    all_to_all x1, blocking collectives: 17 us -> 16.5 us  [on_device(): pieces = lax.all_to_all(partial_sums, 'animal', 0, 0)]
  transfers between devices with their start and end apart: 6 -> 6, of which waited for: 3 -> 3; matrix products, arithmetic and copies ran while one was open for 0% -> 1% of each run, Pallas kernels for 18% -> 18%
where the time goes in v5:
time: 48 us; the launch traced here: 47.8 us
  Pallas kernels  16.8 us (35%)
  blocking collectives  16.5 us (34%)
  starting transfers between devices  9.97 us (21%)
  waiting for transfers between devices  3.4 us (7%)
  between operations  0.74 us (2%)
    all_to_all x1, blocking collectives, on_device(): pieces = lax.all_to_all(partial_sums, 'animal', 0, 0)  16.5 us
    pallas_call x4, Pallas kernels, projection(): pl.pallas_call(functools.partial(projection_kernel, block, ahead[step], N...  15.1 us
    ppermute x1, starting transfers between devices, on_device(): from_chip = lax.ppermute(to_chip, 'marker', OTHER_CHIP)  3.76 us
    ppermute x1, starting transfers between devices, on_device(): there = lax.ppermute(here, 'marker', OTHER_CHIP)  2.39 us
    ppermute x1, waiting for transfers between devices, on_device(): there = lax.ppermute(here, 'marker', OTHER_CHIP)  1.96 us
    ppermute x1, starting transfers between devices, on_device(): other = lax.ppermute(own, 'marker', OTHER_CORE)  1.65 us
    ppermute x1, starting transfers between devices, on_device(): received = lax.ppermute(to_core, 'marker', OTHER_CORE)  1.5 us
  transfers between devices with their start and end apart: 6, of which 3 were waited for; matrix products, arithmetic and copies ran while one was open for 1% of the time, Pallas kernels for 18%

profile of v5, /device:TPU:1, one launch (start us, length us, event | category | flops | bytes accessed | tf_op | source)
XLA Modules:
  0.0 47.8 jit_solution(1114536383738303721)
XLA Ops:
  0.6 6.8 %projection_block_0.1 = (s16[192,512]{1,0:T(8,128)(2,1)S(1)}, bf16[8192,512]{1,0:T(8,128)(2,1)S(1)}, s32[192,6144]{1,0:T(8,128)S(1)}) custom-call(s32[768,8192]{1,0:T(8,128)} %refs_0_.7, bf16[8192,512]{1,0:T(8,128)(2,1)} %refs_1_.1), custom_call_target="tpu_custom_call" | custom-call | flops 1610612736 | bytes 14680064 | tf_op jit(solution)/shard_map/projection_block_0/pallas_call | solution.py:109
  7.4 1.5 %collective-permute-start = (s16[192,512]{1,0:T(8,128)(2,1)S(1)}, s16[192,512]{1,0:T(8,128)(2,1)S(1)}, u32[]{:S(2)}, u32[]{:S(2)}) collective-permute-start(s16[192,512]{1,0:T(8,128)(2,1)S(1)} %get-tuple-element.11.refs_3_), channel_id=1, source_target_pairs={{0,32},{32,0},{64,96},{96,64},{1,33},{33,1},{65,97},{97,65},{2,34}... | collective-permute-start | bytes 589832 | tf_op jit(solution)/shard_map/ppermute | solution.py:212
  8.9 2.1 %projection_block_1.1 = (s16[192,512]{1,0:T(8,128)(2,1)S(1)}, s32[192,2048]{1,0:T(8,128)S(1)}) custom-call(s32[768,8192]{1,0:T(8,128)} %refs_0_.7, bf16[8192,512]{1,0:T(8,128)(2,1)S(1)} %get-tuple-element.9.refs_1_, s32[192,6144]{1,0:T(8,128)S(1)} %get-tuple-element.10.refs_2_, s16[192,512]{1,0:T(8,128)(2,1)S(1)} %get-tuple-element.11.refs_3_), custom_call_target="tpu_custom_call" | custom-call | flops 1610612736 | bytes 6291456 | tf_op jit(solution)/shard_map/projection_block_1/pallas_call | solution.py:109
  11.0 0.0 collective-permute-done
  11.0 0.1 add.6.refs_3_
  11.1 3.8 %collective-permute-start.1 = (s16[192,512]{1,0:T(8,128)(2,1)S(1)}, s16[192,512]{1,0:T(8,128)(2,1)S(1)}, u32[]{:S(2)}, u32[]{:S(2)}) collective-permute-start(s16[192,512]{1,0:T(8,128)(2,1)S(1)} %add.6.refs_3_), channel_id=1, source_target_pairs={{0,64},{64,0},{32,96},{96,32},{1,65},{65,1},{33,97},{97,33},{2,66}... | collective-permute-start | bytes 589832 | tf_op jit(solution)/shard_map/ppermute | solution.py:215
  14.9 3.5 %projection_block_2.1 = (s16[192,512]{1,0:T(8,128)(2,1)S(1)}, s32[192,4096]{1,0:T(8,128)S(1)}) custom-call(s32[768,8192]{1,0:T(8,128)} %refs_0_.7, bf16[8192,512]{1,0:T(8,128)(2,1)S(1)} %get-tuple-element.9.refs_1_, s32[192,2048]{1,0:T(8,128)S(1)} %get-tuple-element.12.refs_2_, s16[192,512]{1,0:T(8,128)(2,1)S(1)} %add.6.refs_3_), custom_call_target="tpu_custom_call" | custom-call | flops 1610612736 | bytes 6291456 | tf_op jit(solution)/shard_map/projection_block_2/pallas_call | solution.py:109
  18.4 0.4 collective-permute-start.2
  18.7 0.0 copy-start
  18.7 0.0 copy-start.1
  18.7 2.8 %projection_block_3.1 = s16[192,512]{1,0:T(8,128)(2,1)S(1)} custom-call(s32[768,8192]{1,0:T(8,128)} %refs_0_.7, bf16[8192,512]{1,0:T(8,128)(2,1)S(1)} %get-tuple-element.9.refs_1_, s32[192,4096]{1,0:T(8,128)S(1)} %get-tuple-element.14.refs_2_, s16[192,512]{1,0:T(8,128)(2,1)S(1)} %get-tuple-element.15.refs_3_), custom_call_target="tpu_custom_call" | custom-call | flops 1610612736 | bytes 6291456 | tf_op jit(solution)/shard_map/projection_block_3/pallas_call | solution.py:109
  21.5 0.0 collective-permute-done.1
  21.5 0.1 add.7.kept_ref
  21.6 0.0 collective-permute-done.2.core_ref
  21.6 0.0 copy-done
  21.6 0.3 features.1.feature_ref
  21.9 0.3 collective-permute-start.3
  22.2 0.0 copy-done.1
  22.2 0.2 copy.6
  22.4 0.1 pad_maximum_fusion.pheno_ref
  22.5 0.3 gram_cross.2.refs_0_
  22.8 0.6 %collective-permute-done.3.feature_ref = bf16[192,512]{1,0:T(8,128)(2,1)S(1)} collective-permute-done((bf16[192,512]{1,0:T(8,128)(2,1)S(1)}, bf16[192,512]{1,0:T(8,128)(2,1)S(1)}, u32[]{:S(2)}, u32[]{:S(2)}) %collective-permute-start.3) | collective-permute-done | bytes 196640 | tf_op jit(solution)/shard_map/ppermute | solution.py:227
  23.4 0.3 gram_cross.3
  23.8 16.5 %all_to_all.5.in_ref = bf16[32,40,128]{2,1,0:T(8,128)(2,1)S(1)} all-to-all(bf16[32,40,128]{2,1,0:T(8,128)(2,1)S(1)} %gram_cross.3), channel_id=1, replica_groups=mesh['marker'=4,'animal'=32] {'animal'}, dimensions={0} | all-to-all | bytes 655360 | tf_op jit(solution)/shard_map/all_to_all | solution.py:248
  40.2 0.1 sum_animals.1.own_ref
  40.3 1.6 %collective-permute-start.4 = (f32[40,128]{1,0:T(8,128)S(1)}, f32[40,128]{1,0:T(8,128)S(1)}, u32[]{:S(2)}, u32[]{:S(2)}) collective-permute-start(f32[40,128]{1,0:T(8,128)S(1)} %sum_animals.1.own_ref), channel_id=1, source_target_pairs={{0,32},{32,0},{64,96},{96,64},{1,33},{33,1},{65,97},{97,65},{2,34}... | collective-permute-start | bytes 61448 | tf_op jit(solution)/shard_map/ppermute | solution.py:257
  41.9 0.8 %collective-permute-done.4.other_ref = f32[40,128]{1,0:T(8,128)S(1)} collective-permute-done((f32[40,128]{1,0:T(8,128)S(1)}, f32[40,128]{1,0:T(8,128)S(1)}, u32[]{:S(2)}, u32[]{:S(2)}) %collective-permute-start.4) | collective-permute-done | bytes 20512 | tf_op jit(solution)/shard_map/ppermute | solution.py:257
  42.8 2.4 %collective-permute-start.5 = (f32[2,40,128]{2,1,0:T(8,128)S(1)}, f32[2,40,128]{2,1,0:T(8,128)S(1)}, u32[]{:S(2)}, u32[]{:S(2)}) collective-permute-start(f32[2,40,128]{2,1,0:T(8,128)S(1)} %join_cores.1.here_ref), channel_id=1, source_target_pairs={{0,64},{64,0},{32,96},{96,32},{1,65},{65,1},{33,97},{97,33},{2,66}... | collective-permute-start | bytes 122888 | tf_op jit(solution)/shard_map/ppermute | solution.py:266
  45.2 2.0 %collective-permute-done.5.there_ref = f32[2,40,128]{2,1,0:T(8,128)S(1)} collective-permute-done((f32[2,40,128]{2,1,0:T(8,128)S(1)}, f32[2,40,128]{2,1,0:T(8,128)S(1)}, u32[]{:S(2)}, u32[]{:S(2)}) %collective-permute-start.5) | collective-permute-done | bytes 40992 | tf_op jit(solution)/shard_map/ppermute | solution.py:266
  47.1 0.7 %finish.1 = (f32[16,512]{1,0:T(8,128)}, f32[16,64]{1,0:T(8,128)}) custom-call(f32[2,40,128]{2,1,0:T(8,128)S(1)} %join_cores.1.here_ref, f32[2,40,128]{2,1,0:T(8,128)S(1)} %collective-permute-done.5.there_ref), custom_call_target="tpu_custom_call" | custom-call | tf_op jit(solution)/shard_map/finish/pallas_call | solution.py:268
  (1 shorter events, 0.0 us)
Async XLA Ops:
  7.4 3.6 %collective-permute-start = (s16[192,512]{1,0:T(8,128)(2,1)S(1)}, s16[192,512]{1,0:T(8,128)(2,1)S(1)}, u32[]{:S(2)}, u32[]{:S(2)}) collective-permute-start(s16[192,512]{1,0:T(8,128)(2,1)S(1)} %get-tuple-element.11.refs_3_), channel_id=1, source_target_pairs={{0,32},{32,0},{64,96},{96,64},{1,33},{33,1},{65,97},{97,65},{2,34}... | collective-permute-start | bytes 589832 | tf_op jit(solution)/shard_map/ppermute | solution.py:212
  11.1 10.4 %collective-permute-start.1 = (s16[192,512]{1,0:T(8,128)(2,1)S(1)}, s16[192,512]{1,0:T(8,128)(2,1)S(1)}, u32[]{:S(2)}, u32[]{:S(2)}) collective-permute-start(s16[192,512]{1,0:T(8,128)(2,1)S(1)} %add.6.refs_3_), channel_id=1, source_target_pairs={{0,64},{64,0},{32,96},{96,32},{1,65},{65,1},{33,97},{97,33},{2,66}... | collective-permute-start | bytes 589832 | tf_op jit(solution)/shard_map/ppermute | solution.py:215
  18.4 3.2 %collective-permute-start.2 = (s16[192,512]{1,0:T(8,128)(2,1)S(1)}, s16[192,512]{1,0:T(8,128)(2,1)S(1)}, u32[]{:S(2)}, u32[]{:S(2)}) collective-permute-start(s16[192,512]{1,0:T(8,128)(2,1)S(1)} %get-tuple-element.15.refs_3_), channel_id=1, source_target_pairs={{0,32},{32,0},{64,96},{96,64},{1,33},{33,1},{65,97},{97,65},{2,34}... | collective-permute-start | bytes 589832 | tf_op jit(solution)/shard_map/ppermute | solution.py:217
  18.7 2.9 %copy-start = (f32[512]{0:T(512)S(1)}, f32[512]{0:T(512)}, u32[]{:S(2)}) copy-start(f32[512]{0:T(512)} %param.6) | copy-start | bytes 6148
  18.7 3.5 %copy-start.1 = (bf16[768,64]{0,1:T(8,128)(2,1)S(1)}, bf16[768,64]{0,1:T(8,128)(2,1)}, u32[]{:S(2)}) copy-start(bf16[768,64]{0,1:T(8,128)(2,1)} %param.7) | copy-start | bytes 294916
  21.9 1.5 %collective-permute-start.3 = (bf16[192,512]{1,0:T(8,128)(2,1)S(1)}, bf16[192,512]{1,0:T(8,128)(2,1)S(1)}, u32[]{:S(2)}, u32[]{:S(2)}) collective-permute-start(bf16[192,512]{1,0:T(8,128)(2,1)S(1)} %features.1.feature_ref), channel_id=1, source_target_pairs={{0,32},{32,0},{64,96},{96,64},{1,33},{33,1},{65,97},{97,65},{2,34}... | collective-permute-start | bytes 589832 | tf_op jit(solution)/shard_map/ppermute | solution.py:227
  40.3 2.5 %collective-permute-start.4 = (f32[40,128]{1,0:T(8,128)S(1)}, f32[40,128]{1,0:T(8,128)S(1)}, u32[]{:S(2)}, u32[]{:S(2)}) collective-permute-start(f32[40,128]{1,0:T(8,128)S(1)} %sum_animals.1.own_ref), channel_id=1, source_target_pairs={{0,32},{32,0},{64,96},{96,64},{1,33},{33,1},{65,97},{97,65},{2,34}... | collective-permute-start | bytes 61448 | tf_op jit(solution)/shard_map/ppermute | solution.py:257
  42.8 4.4 %collective-permute-start.5 = (f32[2,40,128]{2,1,0:T(8,128)S(1)}, f32[2,40,128]{2,1,0:T(8,128)S(1)}, u32[]{:S(2)}, u32[]{:S(2)}) collective-permute-start(f32[2,40,128]{2,1,0:T(8,128)S(1)} %join_cores.1.here_ref), channel_id=1, source_target_pairs={{0,64},{64,0},{32,96},{96,32},{1,65},{65,1},{33,97},{97,33},{2,66}... | collective-permute-start | bytes 122888 | tf_op jit(solution)/shard_map/ppermute | solution.py:266

commit v6 on v5

--- a/solution.py
+++ b/solution.py
@@ -161,9 +161,8 @@
     cross = jnp.where(left, cross[:, 0], cross[:, 1])
     high = cross.astype(jnp.bfloat16)
     low = (cross - high.astype(jnp.float32)).astype(jnp.bfloat16)
-    out_ref[:, :height] = gram[:, :LANES].reshape(pieces, height, LANES)
-    out_ref[:, height : 2 * height] = gram[:, LANES:].reshape(pieces, height, LANES)
-    out_ref[:, 2 * height :] = jnp.where(core == 0, high, low)
+    halves = [gram[:, start : start + LANES].reshape(pieces, height, LANES) for start in (0, LANES)]
+    out_ref[...] = jnp.concatenate(halves + [jnp.where(core == 0, high, low)], axis=1)
 
 
 def sum_kernel(in_ref, out_ref):

time: 48 us -> 48 us (level)
  no operation moved by 1% of the time
where the time goes in v6:
time: 48 us; the launch traced here: 47.8 us
  Pallas kernels  16.9 us (35%)
  blocking collectives  16.5 us (34%)
  starting transfers between devices  9.97 us (21%)
  waiting for transfers between devices  3.4 us (7%)
  between operations  0.74 us (2%)
    all_to_all x1, blocking collectives, on_device(): pieces = lax.all_to_all(partial_sums, 'animal', 0, 0)  16.5 us
    pallas_call x4, Pallas kernels, projection(): pl.pallas_call(functools.partial(projection_kernel, block, ahead[step], N...  15.1 us
    ppermute x1, starting transfers between devices, on_device(): from_chip = lax.ppermute(to_chip, 'marker', OTHER_CHIP)  3.76 us
    ppermute x1, starting transfers between devices, on_device(): there = lax.ppermute(here, 'marker', OTHER_CHIP)  2.39 us
    ppermute x1, waiting for transfers between devices, on_device(): there = lax.ppermute(here, 'marker', OTHER_CHIP)  1.96 us
    ppermute x1, starting transfers between devices, on_device(): other = lax.ppermute(own, 'marker', OTHER_CORE)  1.65 us
    ppermute x1, starting transfers between devices, on_device(): received = lax.ppermute(to_core, 'marker', OTHER_CORE)  1.5 us
  transfers between devices with their start and end apart: 6, of which 3 were waited for; matrix products, arithmetic and copies ran while one was open for 1% of the time, Pallas kernels for 18%

profile of v6, /device:TPU:1, one launch (start us, length us, event | category | flops | bytes accessed | tf_op | source)
XLA Modules:
  0.0 47.8 jit_solution(5144824649648854484)
XLA Ops:
  0.6 6.8 %projection_block_0.1 = (s16[192,512]{1,0:T(8,128)(2,1)S(1)}, bf16[8192,512]{1,0:T(8,128)(2,1)S(1)}, s32[192,6144]{1,0:T(8,128)S(1)}) custom-call(s32[768,8192]{1,0:T(8,128)} %refs_0_.7, bf16[8192,512]{1,0:T(8,128)(2,1)} %refs_1_.1), custom_call_target="tpu_custom_call" | custom-call | flops 1610612736 | bytes 14680064 | tf_op jit(solution)/shard_map/projection_block_0/pallas_call | solution.py:109
  7.4 1.5 %collective-permute-start = (s16[192,512]{1,0:T(8,128)(2,1)S(1)}, s16[192,512]{1,0:T(8,128)(2,1)S(1)}, u32[]{:S(2)}, u32[]{:S(2)}) collective-permute-start(s16[192,512]{1,0:T(8,128)(2,1)S(1)} %get-tuple-element.11.refs_3_), channel_id=1, source_target_pairs={{0,32},{32,0},{64,96},{96,64},{1,33},{33,1},{65,97},{97,65},{2,34}... | collective-permute-start | bytes 589832 | tf_op jit(solution)/shard_map/ppermute | solution.py:211
  8.9 2.1 %projection_block_1.1 = (s16[192,512]{1,0:T(8,128)(2,1)S(1)}, s32[192,2048]{1,0:T(8,128)S(1)}) custom-call(s32[768,8192]{1,0:T(8,128)} %refs_0_.7, bf16[8192,512]{1,0:T(8,128)(2,1)S(1)} %get-tuple-element.9.refs_1_, s32[192,6144]{1,0:T(8,128)S(1)} %get-tuple-element.10.refs_2_, s16[192,512]{1,0:T(8,128)(2,1)S(1)} %get-tuple-element.11.refs_3_), custom_call_target="tpu_custom_call" | custom-call | flops 1610612736 | bytes 6291456 | tf_op jit(solution)/shard_map/projection_block_1/pallas_call | solution.py:109
  11.0 0.0 collective-permute-done
  11.0 0.1 add.6.refs_3_
  11.1 3.8 %collective-permute-start.1 = (s16[192,512]{1,0:T(8,128)(2,1)S(1)}, s16[192,512]{1,0:T(8,128)(2,1)S(1)}, u32[]{:S(2)}, u32[]{:S(2)}) collective-permute-start(s16[192,512]{1,0:T(8,128)(2,1)S(1)} %add.6.refs_3_), channel_id=1, source_target_pairs={{0,64},{64,0},{32,96},{96,32},{1,65},{65,1},{33,97},{97,33},{2,66}... | collective-permute-start | bytes 589832 | tf_op jit(solution)/shard_map/ppermute | solution.py:214
  14.9 3.5 %projection_block_2.1 = (s16[192,512]{1,0:T(8,128)(2,1)S(1)}, s32[192,4096]{1,0:T(8,128)S(1)}) custom-call(s32[768,8192]{1,0:T(8,128)} %refs_0_.7, bf16[8192,512]{1,0:T(8,128)(2,1)S(1)} %get-tuple-element.9.refs_1_, s32[192,2048]{1,0:T(8,128)S(1)} %get-tuple-element.12.refs_2_, s16[192,512]{1,0:T(8,128)(2,1)S(1)} %add.6.refs_3_), custom_call_target="tpu_custom_call" | custom-call | flops 1610612736 | bytes 6291456 | tf_op jit(solution)/shard_map/projection_block_2/pallas_call | solution.py:109
  18.4 0.4 collective-permute-start.2
  18.7 0.0 copy-start
  18.7 0.0 copy-start.1
  18.7 2.8 %projection_block_3.1 = s16[192,512]{1,0:T(8,128)(2,1)S(1)} custom-call(s32[768,8192]{1,0:T(8,128)} %refs_0_.7, bf16[8192,512]{1,0:T(8,128)(2,1)S(1)} %get-tuple-element.9.refs_1_, s32[192,4096]{1,0:T(8,128)S(1)} %get-tuple-element.14.refs_2_, s16[192,512]{1,0:T(8,128)(2,1)S(1)} %get-tuple-element.15.refs_3_), custom_call_target="tpu_custom_call" | custom-call | flops 1610612736 | bytes 6291456 | tf_op jit(solution)/shard_map/projection_block_3/pallas_call | solution.py:109
  21.5 0.0 collective-permute-done.1
  21.5 0.1 add.7.kept_ref
  21.6 0.0 collective-permute-done.2.core_ref
  21.6 0.0 copy-done
  21.6 0.3 features.1.feature_ref
  21.9 0.3 collective-permute-start.3
  22.2 0.0 copy-done.1
  22.2 0.2 copy.6
  22.4 0.1 pad_maximum_fusion.pheno_ref
  22.5 0.3 gram_cross.2.refs_0_
  22.8 0.6 %collective-permute-done.3.feature_ref = bf16[192,512]{1,0:T(8,128)(2,1)S(1)} collective-permute-done((bf16[192,512]{1,0:T(8,128)(2,1)S(1)}, bf16[192,512]{1,0:T(8,128)(2,1)S(1)}, u32[]{:S(2)}, u32[]{:S(2)}) %collective-permute-start.3) | collective-permute-done | bytes 196640 | tf_op jit(solution)/shard_map/ppermute | solution.py:226
  23.4 0.3 gram_cross.3
  23.8 16.5 %all_to_all.5.in_ref = bf16[32,40,128]{2,1,0:T(8,128)(2,1)S(1)} all-to-all(bf16[32,40,128]{2,1,0:T(8,128)(2,1)S(1)} %gram_cross.3), channel_id=1, replica_groups=mesh['marker'=4,'animal'=32] {'animal'}, dimensions={0} | all-to-all | bytes 655360 | tf_op jit(solution)/shard_map/all_to_all | solution.py:247
  40.2 0.1 sum_animals.1.own_ref
  40.3 1.6 %collective-permute-start.4 = (f32[40,128]{1,0:T(8,128)S(1)}, f32[40,128]{1,0:T(8,128)S(1)}, u32[]{:S(2)}, u32[]{:S(2)}) collective-permute-start(f32[40,128]{1,0:T(8,128)S(1)} %sum_animals.1.own_ref), channel_id=1, source_target_pairs={{0,32},{32,0},{64,96},{96,64},{1,33},{33,1},{65,97},{97,65},{2,34}... | collective-permute-start | bytes 61448 | tf_op jit(solution)/shard_map/ppermute | solution.py:256
  41.9 0.8 %collective-permute-done.4.other_ref = f32[40,128]{1,0:T(8,128)S(1)} collective-permute-done((f32[40,128]{1,0:T(8,128)S(1)}, f32[40,128]{1,0:T(8,128)S(1)}, u32[]{:S(2)}, u32[]{:S(2)}) %collective-permute-start.4) | collective-permute-done | bytes 20512 | tf_op jit(solution)/shard_map/ppermute | solution.py:256
  42.8 2.4 %collective-permute-start.5 = (f32[2,40,128]{2,1,0:T(8,128)S(1)}, f32[2,40,128]{2,1,0:T(8,128)S(1)}, u32[]{:S(2)}, u32[]{:S(2)}) collective-permute-start(f32[2,40,128]{2,1,0:T(8,128)S(1)} %join_cores.1.here_ref), channel_id=1, source_target_pairs={{0,64},{64,0},{32,96},{96,32},{1,65},{65,1},{33,97},{97,33},{2,66}... | collective-permute-start | bytes 122888 | tf_op jit(solution)/shard_map/ppermute | solution.py:265
  45.2 2.0 %collective-permute-done.5.there_ref = f32[2,40,128]{2,1,0:T(8,128)S(1)} collective-permute-done((f32[2,40,128]{2,1,0:T(8,128)S(1)}, f32[2,40,128]{2,1,0:T(8,128)S(1)}, u32[]{:S(2)}, u32[]{:S(2)}) %collective-permute-start.5) | collective-permute-done | bytes 40992 | tf_op jit(solution)/shard_map/ppermute | solution.py:265
  47.1 0.7 %finish.1 = (f32[16,512]{1,0:T(8,128)}, f32[16,64]{1,0:T(8,128)}) custom-call(f32[2,40,128]{2,1,0:T(8,128)S(1)} %join_cores.1.here_ref, f32[2,40,128]{2,1,0:T(8,128)S(1)} %collective-permute-done.5.there_ref), custom_call_target="tpu_custom_call" | custom-call | tf_op jit(solution)/shard_map/finish/pallas_call | solution.py:267
  (1 shorter events, 0.0 us)
Async XLA Ops:
  7.4 3.6 %collective-permute-start = (s16[192,512]{1,0:T(8,128)(2,1)S(1)}, s16[192,512]{1,0:T(8,128)(2,1)S(1)}, u32[]{:S(2)}, u32[]{:S(2)}) collective-permute-start(s16[192,512]{1,0:T(8,128)(2,1)S(1)} %get-tuple-element.11.refs_3_), channel_id=1, source_target_pairs={{0,32},{32,0},{64,96},{96,64},{1,33},{33,1},{65,97},{97,65},{2,34}... | collective-permute-start | bytes 589832 | tf_op jit(solution)/shard_map/ppermute | solution.py:211
  11.1 10.4 %collective-permute-start.1 = (s16[192,512]{1,0:T(8,128)(2,1)S(1)}, s16[192,512]{1,0:T(8,128)(2,1)S(1)}, u32[]{:S(2)}, u32[]{:S(2)}) collective-permute-start(s16[192,512]{1,0:T(8,128)(2,1)S(1)} %add.6.refs_3_), channel_id=1, source_target_pairs={{0,64},{64,0},{32,96},{96,32},{1,65},{65,1},{33,97},{97,33},{2,66}... | collective-permute-start | bytes 589832 | tf_op jit(solution)/shard_map/ppermute | solution.py:214
  18.4 3.2 %collective-permute-start.2 = (s16[192,512]{1,0:T(8,128)(2,1)S(1)}, s16[192,512]{1,0:T(8,128)(2,1)S(1)}, u32[]{:S(2)}, u32[]{:S(2)}) collective-permute-start(s16[192,512]{1,0:T(8,128)(2,1)S(1)} %get-tuple-element.15.refs_3_), channel_id=1, source_target_pairs={{0,32},{32,0},{64,96},{96,64},{1,33},{33,1},{65,97},{97,65},{2,34}... | collective-permute-start | bytes 589832 | tf_op jit(solution)/shard_map/ppermute | solution.py:216
  18.7 2.9 %copy-start = (f32[512]{0:T(512)S(1)}, f32[512]{0:T(512)}, u32[]{:S(2)}) copy-start(f32[512]{0:T(512)} %param.6) | copy-start | bytes 6148
  18.7 3.5 %copy-start.1 = (bf16[768,64]{0,1:T(8,128)(2,1)S(1)}, bf16[768,64]{0,1:T(8,128)(2,1)}, u32[]{:S(2)}) copy-start(bf16[768,64]{0,1:T(8,128)(2,1)} %param.7) | copy-start | bytes 294916
  21.9 1.5 %collective-permute-start.3 = (bf16[192,512]{1,0:T(8,128)(2,1)S(1)}, bf16[192,512]{1,0:T(8,128)(2,1)S(1)}, u32[]{:S(2)}, u32[]{:S(2)}) collective-permute-start(bf16[192,512]{1,0:T(8,128)(2,1)S(1)} %features.1.feature_ref), channel_id=1, source_target_pairs={{0,32},{32,0},{64,96},{96,64},{1,33},{33,1},{65,97},{97,65},{2,34}... | collective-permute-start | bytes 589832 | tf_op jit(solution)/shard_map/ppermute | solution.py:226
  40.3 2.5 %collective-permute-start.4 = (f32[40,128]{1,0:T(8,128)S(1)}, f32[40,128]{1,0:T(8,128)S(1)}, u32[]{:S(2)}, u32[]{:S(2)}) collective-permute-start(f32[40,128]{1,0:T(8,128)S(1)} %sum_animals.1.own_ref), channel_id=1, source_target_pairs={{0,32},{32,0},{64,96},{96,64},{1,33},{33,1},{65,97},{97,65},{2,34}... | collective-permute-start | bytes 61448 | tf_op jit(solution)/shard_map/ppermute | solution.py:256
  42.8 4.4 %collective-permute-start.5 = (f32[2,40,128]{2,1,0:T(8,128)S(1)}, f32[2,40,128]{2,1,0:T(8,128)S(1)}, u32[]{:S(2)}, u32[]{:S(2)}) collective-permute-start(f32[2,40,128]{2,1,0:T(8,128)S(1)} %join_cores.1.here_ref), channel_id=1, source_target_pairs={{0,64},{64,0},{32,96},{96,32},{1,65},{65,1},{33,97},{97,33},{2,66}... | collective-permute-start | bytes 122888 | tf_op jit(solution)/shard_map/ppermute | solution.py:265

commit v7 on v6

--- a/solution.py
+++ b/solution.py
@@ -67,8 +67,13 @@
             panel_copies[step].start()
         if step >= came_parts:
             geno_copies[step].start()
-    for copy in ahead_copies.values():
-        copy.start()
+    def start_ahead():
+        for copy in ahead_copies.values():
+            copy.start()
+
+    late = 1 if came_parts == 2 else None
+    if late is None:
+        start_ahead()
 
     def run(*sums):
         for step, (start, width) in enumerate(PARTS):
@@ -76,6 +81,8 @@
                 panel_copies[step].wait()
             if step >= came_parts:
                 geno_copies[step].wait()
+            if step == late:
+                start_ahead()
             for tile in range(start, start + width, TILE):
                 source = came_ref if tile < came_cols else geno
                 dosage = (source[:, tile : tile + TILE] - 1).astype(jnp.float32).astype(jnp.bfloat16)
@@ -122,11 +129,9 @@
 
 
 def features_kernel(kept_ref, core_ref, phase_ref, out_ref):
-    turns = kept_ref[...].astype(jnp.int32) + core_ref[...].astype(jnp.int32)
-    turns = ((turns << 16) >> 16).astype(jnp.float32) * (1.0 / 65536.0)
-    turns = turns + phase_ref[...] * (1.0 / (2.0 * math.pi))
-    turns = turns - jnp.round(turns)
-    t = jnp.abs(turns) - 0.25
+    phase = jnp.round(phase_ref[...] * (2.0**32 / (2.0 * math.pi))).astype(jnp.int32)
+    turns = ((kept_ref[...].astype(jnp.int32) + core_ref[...].astype(jnp.int32)) << 16) + phase
+    t = jnp.abs(turns.astype(jnp.float32) * 2.0**-32) - 0.25
     square = t * t
     value = jnp.full_like(t, SINE[-1])
     for factor in SINE[-2::-1]:

time: 48 us -> 48 us (level)
  no operation moved by 1% of the time
where the time goes in v7:
time: 48 us; the launch traced here: 47.8 us
  Pallas kernels  16.8 us (35%)
  blocking collectives  16.4 us (34%)
  starting transfers between devices  9.98 us (21%)
  waiting for transfers between devices  3.41 us (7%)
  between operations  0.74 us (2%)
    all_to_all x1, blocking collectives, on_device(): pieces = lax.all_to_all(partial_sums, 'animal', 0, 0)  16.4 us
    pallas_call x4, Pallas kernels, projection(): pl.pallas_call(functools.partial(projection_kernel, block, ahead[step], N...  15.1 us
    ppermute x1, starting transfers between devices, on_device(): from_chip = lax.ppermute(to_chip, 'marker', OTHER_CHIP)  3.76 us
    ppermute x1, starting transfers between devices, on_device(): there = lax.ppermute(here, 'marker', OTHER_CHIP)  2.39 us
    ppermute x1, waiting for transfers between devices, on_device(): there = lax.ppermute(here, 'marker', OTHER_CHIP)  1.96 us
    ppermute x1, starting transfers between devices, on_device(): other = lax.ppermute(own, 'marker', OTHER_CORE)  1.66 us
    ppermute x1, starting transfers between devices, on_device(): received = lax.ppermute(to_core, 'marker', OTHER_CORE)  1.5 us
  transfers between devices with their start and end apart: 6, of which 3 were waited for; matrix products, arithmetic and copies ran while one was open for 1% of the time, Pallas kernels for 18%

profile of v7, /device:TPU:1, one launch (start us, length us, event | category | flops | bytes accessed | tf_op | source)
XLA Modules:
  0.0 47.8 jit_solution(7288744012323938796)
XLA Ops:
  0.6 6.8 %projection_block_0.1 = (s16[192,512]{1,0:T(8,128)(2,1)S(1)}, bf16[8192,512]{1,0:T(8,128)(2,1)S(1)}, s32[192,6144]{1,0:T(8,128)S(1)}) custom-call(s32[768,8192]{1,0:T(8,128)} %refs_0_.7, bf16[8192,512]{1,0:T(8,128)(2,1)} %refs_1_.1), custom_call_target="tpu_custom_call" | custom-call | flops 1610612736 | bytes 14680064 | tf_op jit(solution)/shard_map/projection_block_0/pallas_call | solution.py:116
  7.4 1.5 %collective-permute-start = (s16[192,512]{1,0:T(8,128)(2,1)S(1)}, s16[192,512]{1,0:T(8,128)(2,1)S(1)}, u32[]{:S(2)}, u32[]{:S(2)}) collective-permute-start(s16[192,512]{1,0:T(8,128)(2,1)S(1)} %get-tuple-element.11.refs_3_), channel_id=1, source_target_pairs={{0,32},{32,0},{64,96},{96,64},{1,33},{33,1},{65,97},{97,65},{2,34}... | collective-permute-start | bytes 589832 | tf_op jit(solution)/shard_map/ppermute | solution.py:216
  8.9 2.1 %projection_block_1.1 = (s16[192,512]{1,0:T(8,128)(2,1)S(1)}, s32[192,2048]{1,0:T(8,128)S(1)}) custom-call(s32[768,8192]{1,0:T(8,128)} %refs_0_.7, bf16[8192,512]{1,0:T(8,128)(2,1)S(1)} %get-tuple-element.9.refs_1_, s32[192,6144]{1,0:T(8,128)S(1)} %get-tuple-element.10.refs_2_, s16[192,512]{1,0:T(8,128)(2,1)S(1)} %get-tuple-element.11.refs_3_), custom_call_target="tpu_custom_call" | custom-call | flops 1610612736 | bytes 6291456 | tf_op jit(solution)/shard_map/projection_block_1/pallas_call | solution.py:116
  11.0 0.0 collective-permute-done
  11.0 0.1 add.6.refs_3_
  11.1 3.8 %collective-permute-start.1 = (s16[192,512]{1,0:T(8,128)(2,1)S(1)}, s16[192,512]{1,0:T(8,128)(2,1)S(1)}, u32[]{:S(2)}, u32[]{:S(2)}) collective-permute-start(s16[192,512]{1,0:T(8,128)(2,1)S(1)} %add.6.refs_3_), channel_id=1, source_target_pairs={{0,64},{64,0},{32,96},{96,32},{1,65},{65,1},{33,97},{97,33},{2,66}... | collective-permute-start | bytes 589832 | tf_op jit(solution)/shard_map/ppermute | solution.py:219
  14.9 3.5 %projection_block_2.1 = (s16[192,512]{1,0:T(8,128)(2,1)S(1)}, s32[192,4096]{1,0:T(8,128)S(1)}) custom-call(s32[768,8192]{1,0:T(8,128)} %refs_0_.7, bf16[8192,512]{1,0:T(8,128)(2,1)S(1)} %get-tuple-element.9.refs_1_, s32[192,2048]{1,0:T(8,128)S(1)} %get-tuple-element.12.refs_2_, s16[192,512]{1,0:T(8,128)(2,1)S(1)} %add.6.refs_3_), custom_call_target="tpu_custom_call" | custom-call | flops 1610612736 | bytes 6291456 | tf_op jit(solution)/shard_map/projection_block_2/pallas_call | solution.py:116
  18.4 0.4 collective-permute-start.2
  18.7 0.0 copy-start
  18.7 0.0 copy-start.1
  18.7 2.8 %projection_block_3.1 = s16[192,512]{1,0:T(8,128)(2,1)S(1)} custom-call(s32[768,8192]{1,0:T(8,128)} %refs_0_.7, bf16[8192,512]{1,0:T(8,128)(2,1)S(1)} %get-tuple-element.9.refs_1_, s32[192,4096]{1,0:T(8,128)S(1)} %get-tuple-element.14.refs_2_, s16[192,512]{1,0:T(8,128)(2,1)S(1)} %get-tuple-element.15.refs_3_), custom_call_target="tpu_custom_call" | custom-call | flops 1610612736 | bytes 6291456 | tf_op jit(solution)/shard_map/projection_block_3/pallas_call | solution.py:116
  21.5 0.0 collective-permute-done.1
  21.5 0.1 add.7.kept_ref
  21.6 0.0 collective-permute-done.2.core_ref
  21.6 0.0 copy-done
  21.6 0.3 features.1.feature_ref
  21.9 0.3 collective-permute-start.3
  22.2 0.0 copy-done.1
  22.2 0.2 copy.6
  22.3 0.1 pad_maximum_fusion.pheno_ref
  22.5 0.3 gram_cross.2.refs_0_
  22.8 0.6 %collective-permute-done.3.feature_ref = bf16[192,512]{1,0:T(8,128)(2,1)S(1)} collective-permute-done((bf16[192,512]{1,0:T(8,128)(2,1)S(1)}, bf16[192,512]{1,0:T(8,128)(2,1)S(1)}, u32[]{:S(2)}, u32[]{:S(2)}) %collective-permute-start.3) | collective-permute-done | bytes 196640 | tf_op jit(solution)/shard_map/ppermute | solution.py:231
  23.4 0.3 gram_cross.3
  23.7 16.4 %all_to_all.5.in_ref = bf16[32,40,128]{2,1,0:T(8,128)(2,1)S(1)} all-to-all(bf16[32,40,128]{2,1,0:T(8,128)(2,1)S(1)} %gram_cross.3), channel_id=1, replica_groups=mesh['marker'=4,'animal'=32] {'animal'}, dimensions={0} | all-to-all | bytes 655360 | tf_op jit(solution)/shard_map/all_to_all | solution.py:252
  40.2 0.1 sum_animals.1.own_ref
  40.2 1.7 %collective-permute-start.4 = (f32[40,128]{1,0:T(8,128)S(1)}, f32[40,128]{1,0:T(8,128)S(1)}, u32[]{:S(2)}, u32[]{:S(2)}) collective-permute-start(f32[40,128]{1,0:T(8,128)S(1)} %sum_animals.1.own_ref), channel_id=1, source_target_pairs={{0,32},{32,0},{64,96},{96,64},{1,33},{33,1},{65,97},{97,65},{2,34}... | collective-permute-start | bytes 61448 | tf_op jit(solution)/shard_map/ppermute | solution.py:261
  41.9 0.8 %collective-permute-done.4.other_ref = f32[40,128]{1,0:T(8,128)S(1)} collective-permute-done((f32[40,128]{1,0:T(8,128)S(1)}, f32[40,128]{1,0:T(8,128)S(1)}, u32[]{:S(2)}, u32[]{:S(2)}) %collective-permute-start.4) | collective-permute-done | bytes 20512 | tf_op jit(solution)/shard_map/ppermute | solution.py:261
  42.8 2.4 %collective-permute-start.5 = (f32[2,40,128]{2,1,0:T(8,128)S(1)}, f32[2,40,128]{2,1,0:T(8,128)S(1)}, u32[]{:S(2)}, u32[]{:S(2)}) collective-permute-start(f32[2,40,128]{2,1,0:T(8,128)S(1)} %join_cores.1.here_ref), channel_id=1, source_target_pairs={{0,64},{64,0},{32,96},{96,32},{1,65},{65,1},{33,97},{97,33},{2,66}... | collective-permute-start | bytes 122888 | tf_op jit(solution)/shard_map/ppermute | solution.py:270
  45.1 2.0 %collective-permute-done.5.there_ref = f32[2,40,128]{2,1,0:T(8,128)S(1)} collective-permute-done((f32[2,40,128]{2,1,0:T(8,128)S(1)}, f32[2,40,128]{2,1,0:T(8,128)S(1)}, u32[]{:S(2)}, u32[]{:S(2)}) %collective-permute-start.5) | collective-permute-done | bytes 40992 | tf_op jit(solution)/shard_map/ppermute | solution.py:270
  47.1 0.7 %finish.1 = (f32[16,512]{1,0:T(8,128)}, f32[16,64]{1,0:T(8,128)}) custom-call(f32[2,40,128]{2,1,0:T(8,128)S(1)} %join_cores.1.here_ref, f32[2,40,128]{2,1,0:T(8,128)S(1)} %collective-permute-done.5.there_ref), custom_call_target="tpu_custom_call" | custom-call | tf_op jit(solution)/shard_map/finish/pallas_call | solution.py:272
  (1 shorter events, 0.0 us)
Async XLA Ops:
  7.4 3.6 %collective-permute-start = (s16[192,512]{1,0:T(8,128)(2,1)S(1)}, s16[192,512]{1,0:T(8,128)(2,1)S(1)}, u32[]{:S(2)}, u32[]{:S(2)}) collective-permute-start(s16[192,512]{1,0:T(8,128)(2,1)S(1)} %get-tuple-element.11.refs_3_), channel_id=1, source_target_pairs={{0,32},{32,0},{64,96},{96,64},{1,33},{33,1},{65,97},{97,65},{2,34}... | collective-permute-start | bytes 589832 | tf_op jit(solution)/shard_map/ppermute | solution.py:216
  11.1 10.4 %collective-permute-start.1 = (s16[192,512]{1,0:T(8,128)(2,1)S(1)}, s16[192,512]{1,0:T(8,128)(2,1)S(1)}, u32[]{:S(2)}, u32[]{:S(2)}) collective-permute-start(s16[192,512]{1,0:T(8,128)(2,1)S(1)} %add.6.refs_3_), channel_id=1, source_target_pairs={{0,64},{64,0},{32,96},{96,32},{1,65},{65,1},{33,97},{97,33},{2,66}... | collective-permute-start | bytes 589832 | tf_op jit(solution)/shard_map/ppermute | solution.py:219
  18.4 3.2 %collective-permute-start.2 = (s16[192,512]{1,0:T(8,128)(2,1)S(1)}, s16[192,512]{1,0:T(8,128)(2,1)S(1)}, u32[]{:S(2)}, u32[]{:S(2)}) collective-permute-start(s16[192,512]{1,0:T(8,128)(2,1)S(1)} %get-tuple-element.15.refs_3_), channel_id=1, source_target_pairs={{0,32},{32,0},{64,96},{96,64},{1,33},{33,1},{65,97},{97,65},{2,34}... | collective-permute-start | bytes 589832 | tf_op jit(solution)/shard_map/ppermute | solution.py:221
  18.7 2.9 %copy-start = (f32[512]{0:T(512)S(1)}, f32[512]{0:T(512)}, u32[]{:S(2)}) copy-start(f32[512]{0:T(512)} %param.6) | copy-start | bytes 6148
  18.7 3.4 %copy-start.1 = (bf16[768,64]{0,1:T(8,128)(2,1)S(1)}, bf16[768,64]{0,1:T(8,128)(2,1)}, u32[]{:S(2)}) copy-start(bf16[768,64]{0,1:T(8,128)(2,1)} %param.7) | copy-start | bytes 294916
  21.9 1.5 %collective-permute-start.3 = (bf16[192,512]{1,0:T(8,128)(2,1)S(1)}, bf16[192,512]{1,0:T(8,128)(2,1)S(1)}, u32[]{:S(2)}, u32[]{:S(2)}) collective-permute-start(bf16[192,512]{1,0:T(8,128)(2,1)S(1)} %features.1.feature_ref), channel_id=1, source_target_pairs={{0,32},{32,0},{64,96},{96,64},{1,33},{33,1},{65,97},{97,65},{2,34}... | collective-permute-start | bytes 589832 | tf_op jit(solution)/shard_map/ppermute | solution.py:231
  40.2 2.5 %collective-permute-start.4 = (f32[40,128]{1,0:T(8,128)S(1)}, f32[40,128]{1,0:T(8,128)S(1)}, u32[]{:S(2)}, u32[]{:S(2)}) collective-permute-start(f32[40,128]{1,0:T(8,128)S(1)} %sum_animals.1.own_ref), channel_id=1, source_target_pairs={{0,32},{32,0},{64,96},{96,64},{1,33},{33,1},{65,97},{97,65},{2,34}... | collective-permute-start | bytes 61448 | tf_op jit(solution)/shard_map/ppermute | solution.py:261
  42.8 4.4 %collective-permute-start.5 = (f32[2,40,128]{2,1,0:T(8,128)S(1)}, f32[2,40,128]{2,1,0:T(8,128)S(1)}, u32[]{:S(2)}, u32[]{:S(2)}) collective-permute-start(f32[2,40,128]{2,1,0:T(8,128)S(1)} %join_cores.1.here_ref), channel_id=1, source_target_pairs={{0,64},{64,0},{32,96},{96,32},{1,65},{65,1},{33,97},{97,33},{2,66}... | collective-permute-start | bytes 122888 | tf_op jit(solution)/shard_map/ppermute | solution.py:270

commit v8 on v7

--- a/solution.py
+++ b/solution.py
@@ -176,18 +176,18 @@
 
 def join_kernel(own_ref, other_ref, out_ref):
     core = lax.axis_index("marker") % 2
-    out_ref[core] = own_ref[...]
-    out_ref[1 - core] = other_ref[...]
+    cross = out_ref.shape[0] - own_ref.shape[0]
+    out_ref[pl.ds(pl.multiple_of(core * cross, cross), cross)] = own_ref[:cross]
+    out_ref[pl.ds(pl.multiple_of((1 - core) * cross, cross), cross)] = other_ref[:cross]
+    out_ref[2 * cross :] = own_ref[cross:] + other_ref[cross:]
 
 
 def finish_kernel(animals_all, here_ref, there_ref, gram_ref, cross_ref):
     height = gram_ref.shape[0]
-    total = here_ref[...] + there_ref[...]
-    for core in range(2):
-        for part in range(2):
-            start = (2 * core + part) * LANES
-            gram_ref[:, start : start + LANES] = total[core, part * height : (part + 1) * height] / animals_all
-    cross = (total[0, 2 * height :] + total[1, 2 * height :]) / math.sqrt(animals_all)
+    for part in range(4):
+        rows = slice(part * height, (part + 1) * height)
+        gram_ref[:, part * LANES : (part + 1) * LANES] = (here_ref[rows] + there_ref[rows]) / animals_all
+    cross = (here_ref[4 * height :] + there_ref[4 * height :]) / math.sqrt(animals_all)
     cross_ref[: height // 2] = cross[:, : LANES // 2]
     cross_ref[height // 2 :] = cross[:, LANES // 2 :]
 
@@ -262,7 +262,7 @@
     with jax.named_scope("join_cores"):
         here = pl.pallas_call(
             join_kernel,
-            out_shape=jax.ShapeDtypeStruct((2,) + own.shape, jnp.float32),
+            out_shape=jax.ShapeDtypeStruct((own.shape[0] + 2 * height, LANES), jnp.float32),
             in_specs=[vmem()] * 2,
             out_specs=vmem(),
             compiler_params=small,

time: 48 us -> 48 us (level)
  no operation moved by 1% of the time
where the time goes in v8:
time: 48 us; the launch traced here: 47.7 us
  Pallas kernels  16.8 us (35%)
  blocking collectives  16.4 us (34%)
  starting transfers between devices  9.98 us (21%)
  waiting for transfers between devices  3.36 us (7%)
  between operations  0.74 us (2%)
    all_to_all x1, blocking collectives, on_device(): pieces = lax.all_to_all(partial_sums, 'animal', 0, 0)  16.4 us
    pallas_call x4, Pallas kernels, projection(): pl.pallas_call(functools.partial(projection_kernel, block, ahead[step], N...  15.1 us
    ppermute x1, starting transfers between devices, on_device(): from_chip = lax.ppermute(to_chip, 'marker', OTHER_CHIP)  3.76 us
    ppermute x1, starting transfers between devices, on_device(): there = lax.ppermute(here, 'marker', OTHER_CHIP)  2.39 us
    ppermute x1, waiting for transfers between devices, on_device(): there = lax.ppermute(here, 'marker', OTHER_CHIP)  1.92 us
    ppermute x1, starting transfers between devices, on_device(): other = lax.ppermute(own, 'marker', OTHER_CORE)  1.66 us
    ppermute x1, starting transfers between devices, on_device(): received = lax.ppermute(to_core, 'marker', OTHER_CORE)  1.5 us
  transfers between devices with their start and end apart: 6, of which 3 were waited for; matrix products, arithmetic and copies ran while one was open for 1% of the time, Pallas kernels for 18%

profile of v8, /device:TPU:1, one launch (start us, length us, event | category | flops | bytes accessed | tf_op | source)
XLA Modules:
  0.0 47.7 jit_solution(12637716069866458847)
XLA Ops:
  0.6 6.8 %projection_block_0.1 = (s16[192,512]{1,0:T(8,128)(2,1)S(1)}, bf16[8192,512]{1,0:T(8,128)(2,1)S(1)}, s32[192,6144]{1,0:T(8,128)S(1)}) custom-call(s32[768,8192]{1,0:T(8,128)} %refs_0_.7, bf16[8192,512]{1,0:T(8,128)(2,1)} %refs_1_.1), custom_call_target="tpu_custom_call" | custom-call | flops 1610612736 | bytes 14680064 | tf_op jit(solution)/shard_map/projection_block_0/pallas_call | solution.py:116
  7.4 1.5 %collective-permute-start = (s16[192,512]{1,0:T(8,128)(2,1)S(1)}, s16[192,512]{1,0:T(8,128)(2,1)S(1)}, u32[]{:S(2)}, u32[]{:S(2)}) collective-permute-start(s16[192,512]{1,0:T(8,128)(2,1)S(1)} %get-tuple-element.11.refs_3_), channel_id=1, source_target_pairs={{0,32},{32,0},{64,96},{96,64},{1,33},{33,1},{65,97},{97,65},{2,34}... | collective-permute-start | bytes 589832 | tf_op jit(solution)/shard_map/ppermute | solution.py:216
  8.9 2.1 %projection_block_1.1 = (s16[192,512]{1,0:T(8,128)(2,1)S(1)}, s32[192,2048]{1,0:T(8,128)S(1)}) custom-call(s32[768,8192]{1,0:T(8,128)} %refs_0_.7, bf16[8192,512]{1,0:T(8,128)(2,1)S(1)} %get-tuple-element.9.refs_1_, s32[192,6144]{1,0:T(8,128)S(1)} %get-tuple-element.10.refs_2_, s16[192,512]{1,0:T(8,128)(2,1)S(1)} %get-tuple-element.11.refs_3_), custom_call_target="tpu_custom_call" | custom-call | flops 1610612736 | bytes 6291456 | tf_op jit(solution)/shard_map/projection_block_1/pallas_call | solution.py:116
  11.0 0.0 collective-permute-done
  11.0 0.1 add.6.refs_3_
  11.1 3.8 %collective-permute-start.1 = (s16[192,512]{1,0:T(8,128)(2,1)S(1)}, s16[192,512]{1,0:T(8,128)(2,1)S(1)}, u32[]{:S(2)}, u32[]{:S(2)}) collective-permute-start(s16[192,512]{1,0:T(8,128)(2,1)S(1)} %add.6.refs_3_), channel_id=1, source_target_pairs={{0,64},{64,0},{32,96},{96,32},{1,65},{65,1},{33,97},{97,33},{2,66}... | collective-permute-start | bytes 589832 | tf_op jit(solution)/shard_map/ppermute | solution.py:219
  14.9 3.5 %projection_block_2.1 = (s16[192,512]{1,0:T(8,128)(2,1)S(1)}, s32[192,4096]{1,0:T(8,128)S(1)}) custom-call(s32[768,8192]{1,0:T(8,128)} %refs_0_.7, bf16[8192,512]{1,0:T(8,128)(2,1)S(1)} %get-tuple-element.9.refs_1_, s32[192,2048]{1,0:T(8,128)S(1)} %get-tuple-element.12.refs_2_, s16[192,512]{1,0:T(8,128)(2,1)S(1)} %add.6.refs_3_), custom_call_target="tpu_custom_call" | custom-call | flops 1610612736 | bytes 6291456 | tf_op jit(solution)/shard_map/projection_block_2/pallas_call | solution.py:116
  18.4 0.4 collective-permute-start.2
  18.7 0.0 copy-start
  18.7 0.0 copy-start.1
  18.7 2.8 %projection_block_3.1 = s16[192,512]{1,0:T(8,128)(2,1)S(1)} custom-call(s32[768,8192]{1,0:T(8,128)} %refs_0_.7, bf16[8192,512]{1,0:T(8,128)(2,1)S(1)} %get-tuple-element.9.refs_1_, s32[192,4096]{1,0:T(8,128)S(1)} %get-tuple-element.14.refs_2_, s16[192,512]{1,0:T(8,128)(2,1)S(1)} %get-tuple-element.15.refs_3_), custom_call_target="tpu_custom_call" | custom-call | flops 1610612736 | bytes 6291456 | tf_op jit(solution)/shard_map/projection_block_3/pallas_call | solution.py:116
  21.5 0.0 collective-permute-done.1
  21.5 0.1 add.7.kept_ref
  21.6 0.0 collective-permute-done.2.core_ref
  21.6 0.0 copy-done
  21.6 0.3 features.1.feature_ref
  21.9 0.3 collective-permute-start.3
  22.2 0.0 copy-done.1
  22.2 0.2 copy.6
  22.3 0.1 pad_maximum_fusion.pheno_ref
  22.5 0.3 gram_cross.2.refs_0_
  22.8 0.6 %collective-permute-done.3.feature_ref = bf16[192,512]{1,0:T(8,128)(2,1)S(1)} collective-permute-done((bf16[192,512]{1,0:T(8,128)(2,1)S(1)}, bf16[192,512]{1,0:T(8,128)(2,1)S(1)}, u32[]{:S(2)}, u32[]{:S(2)}) %collective-permute-start.3) | collective-permute-done | bytes 196640 | tf_op jit(solution)/shard_map/ppermute | solution.py:231
  23.4 0.3 gram_cross.3
  23.7 16.4 %all_to_all.5.in_ref = bf16[32,40,128]{2,1,0:T(8,128)(2,1)S(1)} all-to-all(bf16[32,40,128]{2,1,0:T(8,128)(2,1)S(1)} %gram_cross.3), channel_id=1, replica_groups=mesh['marker'=4,'animal'=32] {'animal'}, dimensions={0} | all-to-all | bytes 655360 | tf_op jit(solution)/shard_map/all_to_all | solution.py:252
  40.2 0.1 sum_animals.1.own_ref
  40.2 1.7 %collective-permute-start.4 = (f32[40,128]{1,0:T(8,128)S(1)}, f32[40,128]{1,0:T(8,128)S(1)}, u32[]{:S(2)}, u32[]{:S(2)}) collective-permute-start(f32[40,128]{1,0:T(8,128)S(1)} %sum_animals.1.own_ref), channel_id=1, source_target_pairs={{0,32},{32,0},{64,96},{96,64},{1,33},{33,1},{65,97},{97,65},{2,34}... | collective-permute-start | bytes 61448 | tf_op jit(solution)/shard_map/ppermute | solution.py:261
  41.9 0.8 %collective-permute-done.4.other_ref = f32[40,128]{1,0:T(8,128)S(1)} collective-permute-done((f32[40,128]{1,0:T(8,128)S(1)}, f32[40,128]{1,0:T(8,128)S(1)}, u32[]{:S(2)}, u32[]{:S(2)}) %collective-permute-start.4) | collective-permute-done | bytes 20512 | tf_op jit(solution)/shard_map/ppermute | solution.py:261
  42.8 2.4 %collective-permute-start.5 = (f32[72,128]{1,0:T(8,128)S(1)}, f32[72,128]{1,0:T(8,128)S(1)}, u32[]{:S(2)}, u32[]{:S(2)}) collective-permute-start(f32[72,128]{1,0:T(8,128)S(1)} %join_cores.1.here_ref), channel_id=1, source_target_pairs={{0,64},{64,0},{32,96},{96,32},{1,65},{65,1},{33,97},{97,33},{2,66}... | collective-permute-start | bytes 110600 | tf_op jit(solution)/shard_map/ppermute | solution.py:270
  45.1 1.9 %collective-permute-done.5.there_ref = f32[72,128]{1,0:T(8,128)S(1)} collective-permute-done((f32[72,128]{1,0:T(8,128)S(1)}, f32[72,128]{1,0:T(8,128)S(1)}, u32[]{:S(2)}, u32[]{:S(2)}) %collective-permute-start.5) | collective-permute-done | bytes 36896 | tf_op jit(solution)/shard_map/ppermute | solution.py:270
  47.1 0.7 %finish.1 = (f32[16,512]{1,0:T(8,128)}, f32[16,64]{1,0:T(8,128)}) custom-call(f32[72,128]{1,0:T(8,128)S(1)} %join_cores.1.here_ref, f32[72,128]{1,0:T(8,128)S(1)} %collective-permute-done.5.there_ref), custom_call_target="tpu_custom_call" | custom-call | tf_op jit(solution)/shard_map/finish/pallas_call | solution.py:272
  (1 shorter events, 0.0 us)
Async XLA Ops:
  7.4 3.6 %collective-permute-start = (s16[192,512]{1,0:T(8,128)(2,1)S(1)}, s16[192,512]{1,0:T(8,128)(2,1)S(1)}, u32[]{:S(2)}, u32[]{:S(2)}) collective-permute-start(s16[192,512]{1,0:T(8,128)(2,1)S(1)} %get-tuple-element.11.refs_3_), channel_id=1, source_target_pairs={{0,32},{32,0},{64,96},{96,64},{1,33},{33,1},{65,97},{97,65},{2,34}... | collective-permute-start | bytes 589832 | tf_op jit(solution)/shard_map/ppermute | solution.py:216
  11.1 10.4 %collective-permute-start.1 = (s16[192,512]{1,0:T(8,128)(2,1)S(1)}, s16[192,512]{1,0:T(8,128)(2,1)S(1)}, u32[]{:S(2)}, u32[]{:S(2)}) collective-permute-start(s16[192,512]{1,0:T(8,128)(2,1)S(1)} %add.6.refs_3_), channel_id=1, source_target_pairs={{0,64},{64,0},{32,96},{96,32},{1,65},{65,1},{33,97},{97,33},{2,66}... | collective-permute-start | bytes 589832 | tf_op jit(solution)/shard_map/ppermute | solution.py:219
  18.4 3.2 %collective-permute-start.2 = (s16[192,512]{1,0:T(8,128)(2,1)S(1)}, s16[192,512]{1,0:T(8,128)(2,1)S(1)}, u32[]{:S(2)}, u32[]{:S(2)}) collective-permute-start(s16[192,512]{1,0:T(8,128)(2,1)S(1)} %get-tuple-element.15.refs_3_), channel_id=1, source_target_pairs={{0,32},{32,0},{64,96},{96,64},{1,33},{33,1},{65,97},{97,65},{2,34}... | collective-permute-start | bytes 589832 | tf_op jit(solution)/shard_map/ppermute | solution.py:221
  18.7 2.9 %copy-start = (f32[512]{0:T(512)S(1)}, f32[512]{0:T(512)}, u32[]{:S(2)}) copy-start(f32[512]{0:T(512)} %param.6) | copy-start | bytes 6148
  18.7 3.4 %copy-start.1 = (bf16[768,64]{0,1:T(8,128)(2,1)S(1)}, bf16[768,64]{0,1:T(8,128)(2,1)}, u32[]{:S(2)}) copy-start(bf16[768,64]{0,1:T(8,128)(2,1)} %param.7) | copy-start | bytes 294916
  21.9 1.5 %collective-permute-start.3 = (bf16[192,512]{1,0:T(8,128)(2,1)S(1)}, bf16[192,512]{1,0:T(8,128)(2,1)S(1)}, u32[]{:S(2)}, u32[]{:S(2)}) collective-permute-start(bf16[192,512]{1,0:T(8,128)(2,1)S(1)} %features.1.feature_ref), channel_id=1, source_target_pairs={{0,32},{32,0},{64,96},{96,64},{1,33},{33,1},{65,97},{97,65},{2,34}... | collective-permute-start | bytes 589832 | tf_op jit(solution)/shard_map/ppermute | solution.py:231
  40.2 2.5 %collective-permute-start.4 = (f32[40,128]{1,0:T(8,128)S(1)}, f32[40,128]{1,0:T(8,128)S(1)}, u32[]{:S(2)}, u32[]{:S(2)}) collective-permute-start(f32[40,128]{1,0:T(8,128)S(1)} %sum_animals.1.own_ref), channel_id=1, source_target_pairs={{0,32},{32,0},{64,96},{96,64},{1,33},{33,1},{65,97},{97,65},{2,34}... | collective-permute-start | bytes 61448 | tf_op jit(solution)/shard_map/ppermute | solution.py:261
  42.8 4.3 %collective-permute-start.5 = (f32[72,128]{1,0:T(8,128)S(1)}, f32[72,128]{1,0:T(8,128)S(1)}, u32[]{:S(2)}, u32[]{:S(2)}) collective-permute-start(f32[72,128]{1,0:T(8,128)S(1)} %join_cores.1.here_ref), channel_id=1, source_target_pairs={{0,64},{64,0},{32,96},{96,32},{1,65},{65,1},{33,97},{97,33},{2,66}... | collective-permute-start | bytes 110600 | tf_op jit(solution)/shard_map/ppermute | solution.py:270

commit v9 on v8

--- a/solution.py
+++ b/solution.py
@@ -186,8 +186,8 @@
     height = gram_ref.shape[0]
     for part in range(4):
         rows = slice(part * height, (part + 1) * height)
-        gram_ref[:, part * LANES : (part + 1) * LANES] = (here_ref[rows] + there_ref[rows]) / animals_all
-    cross = (here_ref[4 * height :] + there_ref[4 * height :]) / math.sqrt(animals_all)
+        gram_ref[:, part * LANES : (part + 1) * LANES] = (here_ref[rows] + there_ref[rows]) * (1.0 / animals_all)
+    cross = (here_ref[4 * height :] + there_ref[4 * height :]) * (1.0 / math.sqrt(animals_all))
     cross_ref[: height // 2] = cross[:, : LANES // 2]
     cross_ref[height // 2 :] = cross[:, LANES // 2 :]
 

time: 48 us -> 48 us (level)
  no operation moved by 1% of the time
where the time goes in v9:
time: 48 us; the launch traced here: 47.7 us
  Pallas kernels  16.8 us (35%)
  blocking collectives  16.4 us (34%)
  starting transfers between devices  9.98 us (21%)
  waiting for transfers between devices  3.36 us (7%)
  between operations  0.74 us (2%)
    all_to_all x1, blocking collectives, on_device(): pieces = lax.all_to_all(partial_sums, 'animal', 0, 0)  16.4 us
    pallas_call x4, Pallas kernels, projection(): pl.pallas_call(functools.partial(projection_kernel, block, ahead[step], N...  15.1 us
    ppermute x1, starting transfers between devices, on_device(): from_chip = lax.ppermute(to_chip, 'marker', OTHER_CHIP)  3.76 us
    ppermute x1, starting transfers between devices, on_device(): there = lax.ppermute(here, 'marker', OTHER_CHIP)  2.39 us
    ppermute x1, waiting for transfers between devices, on_device(): there = lax.ppermute(here, 'marker', OTHER_CHIP)  1.92 us
    ppermute x1, starting transfers between devices, on_device(): other = lax.ppermute(own, 'marker', OTHER_CORE)  1.66 us
    ppermute x1, starting transfers between devices, on_device(): received = lax.ppermute(to_core, 'marker', OTHER_CORE)  1.5 us
  transfers between devices with their start and end apart: 6, of which 3 were waited for; matrix products, arithmetic and copies ran while one was open for 1% of the time, Pallas kernels for 18%

profile of v9, /device:TPU:1, one launch (start us, length us, event | category | flops | bytes accessed | tf_op | source)
XLA Modules:
  0.0 47.7 jit_solution(17746173824932583056)
XLA Ops:
  0.6 6.8 %projection_block_0.1 = (s16[192,512]{1,0:T(8,128)(2,1)S(1)}, bf16[8192,512]{1,0:T(8,128)(2,1)S(1)}, s32[192,6144]{1,0:T(8,128)S(1)}) custom-call(s32[768,8192]{1,0:T(8,128)} %refs_0_.7, bf16[8192,512]{1,0:T(8,128)(2,1)} %refs_1_.1), custom_call_target="tpu_custom_call" | custom-call | flops 1610612736 | bytes 14680064 | tf_op jit(solution)/shard_map/projection_block_0/pallas_call | solution.py:116
  7.4 1.5 %collective-permute-start = (s16[192,512]{1,0:T(8,128)(2,1)S(1)}, s16[192,512]{1,0:T(8,128)(2,1)S(1)}, u32[]{:S(2)}, u32[]{:S(2)}) collective-permute-start(s16[192,512]{1,0:T(8,128)(2,1)S(1)} %get-tuple-element.11.refs_3_), channel_id=1, source_target_pairs={{0,32},{32,0},{64,96},{96,64},{1,33},{33,1},{65,97},{97,65},{2,34}... | collective-permute-start | bytes 589832 | tf_op jit(solution)/shard_map/ppermute | solution.py:216
  8.9 2.1 %projection_block_1.1 = (s16[192,512]{1,0:T(8,128)(2,1)S(1)}, s32[192,2048]{1,0:T(8,128)S(1)}) custom-call(s32[768,8192]{1,0:T(8,128)} %refs_0_.7, bf16[8192,512]{1,0:T(8,128)(2,1)S(1)} %get-tuple-element.9.refs_1_, s32[192,6144]{1,0:T(8,128)S(1)} %get-tuple-element.10.refs_2_, s16[192,512]{1,0:T(8,128)(2,1)S(1)} %get-tuple-element.11.refs_3_), custom_call_target="tpu_custom_call" | custom-call | flops 1610612736 | bytes 6291456 | tf_op jit(solution)/shard_map/projection_block_1/pallas_call | solution.py:116
  11.0 0.0 collective-permute-done
  11.0 0.1 add.6.refs_3_
  11.1 3.8 %collective-permute-start.1 = (s16[192,512]{1,0:T(8,128)(2,1)S(1)}, s16[192,512]{1,0:T(8,128)(2,1)S(1)}, u32[]{:S(2)}, u32[]{:S(2)}) collective-permute-start(s16[192,512]{1,0:T(8,128)(2,1)S(1)} %add.6.refs_3_), channel_id=1, source_target_pairs={{0,64},{64,0},{32,96},{96,32},{1,65},{65,1},{33,97},{97,33},{2,66}... | collective-permute-start | bytes 589832 | tf_op jit(solution)/shard_map/ppermute | solution.py:219
  14.9 3.5 %projection_block_2.1 = (s16[192,512]{1,0:T(8,128)(2,1)S(1)}, s32[192,4096]{1,0:T(8,128)S(1)}) custom-call(s32[768,8192]{1,0:T(8,128)} %refs_0_.7, bf16[8192,512]{1,0:T(8,128)(2,1)S(1)} %get-tuple-element.9.refs_1_, s32[192,2048]{1,0:T(8,128)S(1)} %get-tuple-element.12.refs_2_, s16[192,512]{1,0:T(8,128)(2,1)S(1)} %add.6.refs_3_), custom_call_target="tpu_custom_call" | custom-call | flops 1610612736 | bytes 6291456 | tf_op jit(solution)/shard_map/projection_block_2/pallas_call | solution.py:116
  18.4 0.4 collective-permute-start.2
  18.7 0.0 copy-start
  18.7 0.0 copy-start.1
  18.7 2.8 %projection_block_3.1 = s16[192,512]{1,0:T(8,128)(2,1)S(1)} custom-call(s32[768,8192]{1,0:T(8,128)} %refs_0_.7, bf16[8192,512]{1,0:T(8,128)(2,1)S(1)} %get-tuple-element.9.refs_1_, s32[192,4096]{1,0:T(8,128)S(1)} %get-tuple-element.14.refs_2_, s16[192,512]{1,0:T(8,128)(2,1)S(1)} %get-tuple-element.15.refs_3_), custom_call_target="tpu_custom_call" | custom-call | flops 1610612736 | bytes 6291456 | tf_op jit(solution)/shard_map/projection_block_3/pallas_call | solution.py:116
  21.5 0.0 collective-permute-done.1
  21.5 0.1 add.7.kept_ref
  21.6 0.0 collective-permute-done.2.core_ref
  21.6 0.0 copy-done
  21.6 0.3 features.1.feature_ref
  21.9 0.3 collective-permute-start.3
  22.2 0.0 copy-done.1
  22.2 0.2 copy.6
  22.3 0.1 pad_maximum_fusion.pheno_ref
  22.5 0.3 gram_cross.2.refs_0_
  22.8 0.6 %collective-permute-done.3.feature_ref = bf16[192,512]{1,0:T(8,128)(2,1)S(1)} collective-permute-done((bf16[192,512]{1,0:T(8,128)(2,1)S(1)}, bf16[192,512]{1,0:T(8,128)(2,1)S(1)}, u32[]{:S(2)}, u32[]{:S(2)}) %collective-permute-start.3) | collective-permute-done | bytes 196640 | tf_op jit(solution)/shard_map/ppermute | solution.py:231
  23.4 0.3 gram_cross.3
  23.7 16.4 %all_to_all.5.in_ref = bf16[32,40,128]{2,1,0:T(8,128)(2,1)S(1)} all-to-all(bf16[32,40,128]{2,1,0:T(8,128)(2,1)S(1)} %gram_cross.3), channel_id=1, replica_groups=mesh['marker'=4,'animal'=32] {'animal'}, dimensions={0} | all-to-all | bytes 655360 | tf_op jit(solution)/shard_map/all_to_all | solution.py:252
  40.2 0.1 sum_animals.1.own_ref
  40.2 1.7 %collective-permute-start.4 = (f32[40,128]{1,0:T(8,128)S(1)}, f32[40,128]{1,0:T(8,128)S(1)}, u32[]{:S(2)}, u32[]{:S(2)}) collective-permute-start(f32[40,128]{1,0:T(8,128)S(1)} %sum_animals.1.own_ref), channel_id=1, source_target_pairs={{0,32},{32,0},{64,96},{96,64},{1,33},{33,1},{65,97},{97,65},{2,34}... | collective-permute-start | bytes 61448 | tf_op jit(solution)/shard_map/ppermute | solution.py:261
  41.9 0.8 %collective-permute-done.4.other_ref = f32[40,128]{1,0:T(8,128)S(1)} collective-permute-done((f32[40,128]{1,0:T(8,128)S(1)}, f32[40,128]{1,0:T(8,128)S(1)}, u32[]{:S(2)}, u32[]{:S(2)}) %collective-permute-start.4) | collective-permute-done | bytes 20512 | tf_op jit(solution)/shard_map/ppermute | solution.py:261
  42.8 2.4 %collective-permute-start.5 = (f32[72,128]{1,0:T(8,128)S(1)}, f32[72,128]{1,0:T(8,128)S(1)}, u32[]{:S(2)}, u32[]{:S(2)}) collective-permute-start(f32[72,128]{1,0:T(8,128)S(1)} %join_cores.1.here_ref), channel_id=1, source_target_pairs={{0,64},{64,0},{32,96},{96,32},{1,65},{65,1},{33,97},{97,33},{2,66}... | collective-permute-start | bytes 110600 | tf_op jit(solution)/shard_map/ppermute | solution.py:270
  45.1 1.9 %collective-permute-done.5.there_ref = f32[72,128]{1,0:T(8,128)S(1)} collective-permute-done((f32[72,128]{1,0:T(8,128)S(1)}, f32[72,128]{1,0:T(8,128)S(1)}, u32[]{:S(2)}, u32[]{:S(2)}) %collective-permute-start.5) | collective-permute-done | bytes 36896 | tf_op jit(solution)/shard_map/ppermute | solution.py:270
  47.1 0.7 %finish.1 = (f32[16,512]{1,0:T(8,128)}, f32[16,64]{1,0:T(8,128)}) custom-call(f32[72,128]{1,0:T(8,128)S(1)} %join_cores.1.here_ref, f32[72,128]{1,0:T(8,128)S(1)} %collective-permute-done.5.there_ref), custom_call_target="tpu_custom_call" | custom-call | tf_op jit(solution)/shard_map/finish/pallas_call | solution.py:272
  (1 shorter events, 0.0 us)
Async XLA Ops:
  7.4 3.6 %collective-permute-start = (s16[192,512]{1,0:T(8,128)(2,1)S(1)}, s16[192,512]{1,0:T(8,128)(2,1)S(1)}, u32[]{:S(2)}, u32[]{:S(2)}) collective-permute-start(s16[192,512]{1,0:T(8,128)(2,1)S(1)} %get-tuple-element.11.refs_3_), channel_id=1, source_target_pairs={{0,32},{32,0},{64,96},{96,64},{1,33},{33,1},{65,97},{97,65},{2,34}... | collective-permute-start | bytes 589832 | tf_op jit(solution)/shard_map/ppermute | solution.py:216
  11.1 10.4 %collective-permute-start.1 = (s16[192,512]{1,0:T(8,128)(2,1)S(1)}, s16[192,512]{1,0:T(8,128)(2,1)S(1)}, u32[]{:S(2)}, u32[]{:S(2)}) collective-permute-start(s16[192,512]{1,0:T(8,128)(2,1)S(1)} %add.6.refs_3_), channel_id=1, source_target_pairs={{0,64},{64,0},{32,96},{96,32},{1,65},{65,1},{33,97},{97,33},{2,66}... | collective-permute-start | bytes 589832 | tf_op jit(solution)/shard_map/ppermute | solution.py:219
  18.4 3.2 %collective-permute-start.2 = (s16[192,512]{1,0:T(8,128)(2,1)S(1)}, s16[192,512]{1,0:T(8,128)(2,1)S(1)}, u32[]{:S(2)}, u32[]{:S(2)}) collective-permute-start(s16[192,512]{1,0:T(8,128)(2,1)S(1)} %get-tuple-element.15.refs_3_), channel_id=1, source_target_pairs={{0,32},{32,0},{64,96},{96,64},{1,33},{33,1},{65,97},{97,65},{2,34}... | collective-permute-start | bytes 589832 | tf_op jit(solution)/shard_map/ppermute | solution.py:221
  18.7 2.9 %copy-start = (f32[512]{0:T(512)S(1)}, f32[512]{0:T(512)}, u32[]{:S(2)}) copy-start(f32[512]{0:T(512)} %param.6) | copy-start | bytes 6148
  18.7 3.4 %copy-start.1 = (bf16[768,64]{0,1:T(8,128)(2,1)S(1)}, bf16[768,64]{0,1:T(8,128)(2,1)}, u32[]{:S(2)}) copy-start(bf16[768,64]{0,1:T(8,128)(2,1)} %param.7) | copy-start | bytes 294916
  21.9 1.5 %collective-permute-start.3 = (bf16[192,512]{1,0:T(8,128)(2,1)S(1)}, bf16[192,512]{1,0:T(8,128)(2,1)S(1)}, u32[]{:S(2)}, u32[]{:S(2)}) collective-permute-start(bf16[192,512]{1,0:T(8,128)(2,1)S(1)} %features.1.feature_ref), channel_id=1, source_target_pairs={{0,32},{32,0},{64,96},{96,64},{1,33},{33,1},{65,97},{97,65},{2,34}... | collective-permute-start | bytes 589832 | tf_op jit(solution)/shard_map/ppermute | solution.py:231
  40.2 2.5 %collective-permute-start.4 = (f32[40,128]{1,0:T(8,128)S(1)}, f32[40,128]{1,0:T(8,128)S(1)}, u32[]{:S(2)}, u32[]{:S(2)}) collective-permute-start(f32[40,128]{1,0:T(8,128)S(1)} %sum_animals.1.own_ref), channel_id=1, source_target_pairs={{0,32},{32,0},{64,96},{96,64},{1,33},{33,1},{65,97},{97,65},{2,34}... | collective-permute-start | bytes 61448 | tf_op jit(solution)/shard_map/ppermute | solution.py:261
  42.8 4.3 %collective-permute-start.5 = (f32[72,128]{1,0:T(8,128)S(1)}, f32[72,128]{1,0:T(8,128)S(1)}, u32[]{:S(2)}, u32[]{:S(2)}) collective-permute-start(f32[72,128]{1,0:T(8,128)S(1)} %join_cores.1.here_ref), channel_id=1, source_target_pairs={{0,64},{64,0},{32,96},{96,32},{1,65},{65,1},{33,97},{97,33},{2,66}... | collective-permute-start | bytes 110600 | tf_op jit(solution)/shard_map/ppermute | solution.py:270
